TPU v7x, 128 devices: a whole 4x4x4 slice. The times are simulated.
128 devices in a mesh: tp: 8 (over y, core), dp: 16 (over z, x).
Axes of the slice: x: 4, y: 4, z: 4, core: 2. Of those that a mesh axis runs over, the one named last changes fastest.
Arguments:
- hidden_rows: bfloat16 [16384, 3, 4096], P('dp', None, 'tp'), may hold values from -6 to 6
- target_rows: bfloat16 [16384, 4096], P('dp', 'tp')
- row_counts: int32 [2048], P('dp'), may hold values from 1 to 8, as said below
- seq_slot: int32 [2048], P('dp'), may hold values from 0 to 2047, as said below
- joining_weight: bfloat16 [3, 4096, 4096], P(None, 'tp'), may hold values from -4 to 4
- norm_gain: float32 [4096], replicated, may hold values from 0.1 to 1.9
Outputs:
- seq_loss: float32 [2048], P('dp')
- serving_weight: bfloat16 [3, 4096, 4096], P(None, ('tp', 'dp'))
- column_scale: float32 [4096], replicated
Inputs may be any that keep to these rules, and one draw needn't show every extreme that they name: `seq_slot`: the slots form owners of 128 slots each (owner = slot // 128); the requests of replica d for one owner hold exactly that owner's slots d * 8 to d * 8 + 7, each once. `row_counts`: one owner, drawn anew, gets 8 rows from every request of every replica. For every other owner, the requests of one replica with slots d * 8 + 2m and d * 8 + 2m + 1 have counts that sum to 8. So every replica uses exactly 544 rows.
All inputs are finite; a program needn't handle non-finite values. Where the computation divides by a largest or mean magnitude, that divisor is 1e-20 or more.
Results may differ from a plain program's by a relative error of at most 0.02.
Values may be sent and summed in bfloat16 or wider, within the bound.
A program may use at most 128 MiB of HBM per device.

v0:
```python
import jax
import jax.numpy as jnp
from jax import lax
from jax.experimental import pallas as pl
from jax.experimental.pallas import tpu as pltpu
from jax.sharding import PartitionSpec as P

learn_rate = 1.0

F32, BF16, I32 = jnp.float32, jnp.bfloat16, jnp.int32
EXACT = lax.Precision.HIGHEST
REQS, MOST, SLOTS, LIVE = 128, 8, 1024, 544
HALF = LIVE // 2
PAD = 640
ALL = 4 * LIVE
BLOCK, PART = 512, 256
FEATS = 384
OUT = 4096
ROWS_OUT = 96
CHUNK = 32


def iota(shape, dim):
    return lax.broadcasted_iota(I32, shape, dim)


def names():
    out = [f"x{j}" for j in (1, 2, 3)] + [f"c{i}" for i in range(4)]
    out += ["h+", "h-", "f+", "f-"] + [f"s{j}" for j in range(1, 8)]
    for h in "zy":
        for s in "+-":
            out += [f"{h}1{s}", f"{h}1f{s}"]
            out += [f"{h}2{s}{b}" for b in range(4)] + [f"{h}2f{s}{b}" for b in range(4)]
    out += [f"d{h}{b}" for h in range(2) for b in range(4)]
    out += [f"g{h}{b}{o}{j}" for h in range(2) for b in range(4) for o in range(2) for j in (1, 2, 3)]
    out += [f"m{j}" for j in range(1, 8)] + [f"n{j}" for j in range(1, 16)]
    return {name: i for i, name in enumerate(out)}


IDS = names()
STEP = (0, 3, 1, 2)


def kernel(
    hid_hbm, tgt_hbm, counts_ref, slots_ref, w_hbm, gain_ref,
    loss_ref, serve_ref, scale_ref,
    hid, tgt, wv, pick, xc, wanted, csend, crecv, part, hrecv, frecv, xg, xgt, df, gs, gr, upd,
    owner, cntr, stc, str_, stat, mx, mxr, dpr, sprd, lsem, ss, rs,
):
    t = lax.axis_index("tp")
    d = lax.axis_index("dp")
    y, c = t // 2, t % 2
    z, x = d // 4, d % 4
    sent = []

    def at(y=y, c=c, z=z, x=x):
        return {"tp": (y % 4) * 2 + c, "dp": (z % 4) * 4 + x % 4}

    sibling = at(c=1 - c)

    def send(name, src, dst, device):
        i = IDS[name]
        copy = pltpu.make_async_remote_copy(
            src_ref=src, dst_ref=dst, send_sem=ss.at[i], recv_sem=rs.at[i],
            device_id=device, device_id_type=pl.DeviceIdType.MESH,
        )
        copy.start()
        sent.append(copy)

    def got(name, ref):
        i = IDS[name]
        pltpu.make_async_remote_copy(
            src_ref=ref, dst_ref=ref, send_sem=ss.at[i], recv_sem=rs.at[i],
            device_id=sibling, device_id_type=pl.DeviceIdType.MESH,
        ).wait_recv()

    loads = [
        pltpu.make_async_copy(hid_hbm, hid, lsem.at[0]),
        pltpu.make_async_copy(tgt_hbm, tgt, lsem.at[1]),
    ]
    for zz in range(4):
        for l in range(3):
            loads.append(
                pltpu.make_async_copy(
                    w_hbm.at[l, pl.ds(zz * 128, 128)],
                    wv.at[pl.ds(zz * FEATS + l * 128, 128)],
                    lsem.at[2 + zz * 3 + l],
                )
            )
    for load in loads:
        load.start()
    barrier = pltpu.get_barrier_semaphore()
    for j in range(1, 8):
        pl.semaphore_signal(
            barrier, inc=1, device_id={"tp": (t + j) % 8, "dp": d}, device_id_type=pl.DeviceIdType.MESH
        )
    for j in range(1, 16):
        pl.semaphore_signal(
            barrier, inc=1, device_id={"tp": t, "dp": (d + j) % 16}, device_id_type=pl.DeviceIdType.MESH
        )

    counts = counts_ref[...].astype(F32)
    counts8 = jnp.broadcast_to(counts, (8, REQS))
    expand = (iota((REQS, SLOTS), 1) // MOST == iota((REQS, SLOTS), 0)).astype(F32)
    before = (iota((REQS, REQS), 0) < iota((REQS, REQS), 1)).astype(F32)
    start8 = jnp.dot(counts8, before, precision=EXACT, preferred_element_type=F32)
    count_slot = jnp.dot(counts8, expand, precision=EXACT, preferred_element_type=F32)
    start_slot = jnp.dot(start8, expand, precision=EXACT, preferred_element_type=F32)
    inside = iota((8, SLOTS), 1) % MOST
    rank8 = (start_slot + 0.5).astype(I32) + inside
    rank8 = jnp.where(inside < (count_slot + 0.5).astype(I32), rank8, -1)
    rank = rank8[0:1, :]
    cntr[...] = jnp.ones_like(cntr)

    @pl.loop(0, LIVE // 272)
    def _(i):
        rows = pl.ds(pl.multiple_of(i * 272, 16), 272)
        hit = iota((272, SLOTS), 0) + i * 272 == rank
        pick[rows, :] = jnp.where(hit, 1.0, 0.0).astype(BF16)

    for load in loads[:2]:
        load.wait()

    @pl.loop(0, LIVE // 272)
    def _(i):
        rows = pl.ds(pl.multiple_of(i * 272, 16), 272)
        chosen = pick[rows, :]
        for l in range(3):
            got_rows = jnp.dot(chosen, hid[l], preferred_element_type=F32).astype(BF16)
            for zz in range(4):
                xc[rows, zz * FEATS + l * 128 : zz * FEATS + (l + 1) * 128] = got_rows[
                    :, zz * 128 : (zz + 1) * 128
                ]
        wanted[rows, :] = jnp.dot(chosen, tgt[...], preferred_element_type=F32).astype(BF16)
        owner[rows, :] = lax.dot_general(
            chosen, expand.astype(BF16), (((1,), (1,)), ((), ())), preferred_element_type=F32
        )

    cntr[:, 0:LIVE] = lax.dot_general(
        count_slot.astype(BF16), pick[...], (((1,), (1,)), ((), ())), preferred_element_type=F32
    )
    pl.semaphore_wait(barrier, 22)

    def feats(zz):
        return pl.ds(pl.multiple_of((zz % 4) * FEATS, 128), FEATS)

    def rows_of(zz):
        return pl.ds(pl.multiple_of((zz % 4) * LIVE, 16), LIVE)

    for j in (1, 2, 3):
        send(f"x{j}", xc.at[:, feats(z + j)], xg.at[rows_of(z), :], at(z=z + j))
    own_copy = pltpu.make_async_copy(xc.at[:, feats(z)], xg.at[rows_of(z), :], lsem.at[14])
    own_copy.start()
    for load in loads[2:]:
        load.wait()

    def forward(yy, core, dst):
        column = ((yy % 4) * 2 + core) * BLOCK

        @pl.loop(0, 2)
        def _(i):
            cols = pl.ds(pl.multiple_of(column + i * PART, PART), PART)
            dst[:, pl.ds(pl.multiple_of(i * PART, PART), PART)] = jnp.dot(
                xc[...], wv[:, cols], preferred_element_type=F32
            ).astype(dst.dtype)

    def to_sibling(i, step):
        forward(y + step, 1 - c, csend.at[i])
        send(f"c{i}", csend.at[i], crecv.at[i], sibling)

    ysend = [hid.at[i, pl.ds(0, LIVE)] for i in range(3)]
    up, down = at(y=y + 1), at(y=y + 3)
    top, low = pl.ds(0, HALF), pl.ds(HALF, HALF)
    to_sibling(0, 2)
    forward(y + 2, c, part.at[0])
    got("c0", crecv.at[0])
    ysend[0][...] = (part[0] + crecv[0].astype(F32)).astype(BF16)
    send("h+", ysend[0].at[top], hrecv.at[0], up)
    send("h-", ysend[0].at[low], hrecv.at[1], down)
    to_sibling(1, 1)
    forward(y + 1, c, part.at[1])
    to_sibling(2, 3)
    forward(y + 3, c, part.at[2])
    got("c1", crecv.at[1])
    got("c2", crecv.at[2])
    got("h+", hrecv.at[0])
    ysend[1][top, :] = (part[1, top, :] + crecv[1, top, :].astype(F32) + hrecv[0].astype(F32)).astype(BF16)
    ysend[1][low, :] = (part[1, low, :] + crecv[1, low, :].astype(F32)).astype(BF16)
    send("f+", ysend[1], frecv.at[0], up)
    got("h-", hrecv.at[1])
    ysend[2][top, :] = (part[2, top, :] + crecv[2, top, :].astype(F32)).astype(BF16)
    ysend[2][low, :] = (part[2, low, :] + crecv[2, low, :].astype(F32) + hrecv[1].astype(F32)).astype(BF16)
    send("f-", ysend[2], frecv.at[1], down)
    to_sibling(3, 0)
    forward(y, c, part.at[0])

    own_copy.wait()
    for j in (1, 2, 3):
        got(f"x{j}", xg.at[rows_of(z + 4 - j), :])

    @pl.loop(0, ALL // 128)
    def _(k):
        places = pl.ds(pl.multiple_of(k * 128, 128), 128)
        turned = xg[places, :].T
        for xx in range(4):
            for l in range(3):
                xgt[xx * ROWS_OUT + l * 32 : xx * ROWS_OUT + (l + 1) * 32, places] = turned[
                    l * 128 + xx * 32 : l * 128 + (xx + 1) * 32, :
                ]

    got("c3", crecv.at[3])
    got("f+", frecv.at[0])
    got("f-", frecv.at[1])
    gain = gain_ref[pl.ds(t, 1), :]
    stc[...] = jnp.zeros_like(stc)
    lane = iota((CHUNK, 128), 1)

    @pl.loop(0, LIVE // CHUNK)
    def _(i):
        rows = pl.ds(pl.multiple_of(i * CHUNK, CHUNK), CHUNK)
        joined = part[0, rows, :] + crecv[3, rows, :].astype(F32)
        joined = joined + (frecv[0, rows, :].astype(F32) + frecv[1, rows, :].astype(F32))
        part[0, rows, :] = joined
        goal = wanted[rows, :].astype(F32)
        scaled = joined * gain
        sums = [joined * joined, scaled * scaled, scaled * goal, goal * goal]
        row = jnp.zeros((CHUNK, 128), F32)
        for k, term in enumerate(sums):
            row = jnp.where(lane == k, jnp.sum(term, axis=1, keepdims=True), row)
        stc[rows, :] = row

    turned = stc[...].T
    stat[pl.ds(t, 1)] = turned[None, 0:8, :]
    for j in range(1, 8):
        send(f"s{j}", stat.at[t], stat.at[t], {"tp": (t + j) % 8, "dp": d})
    for j in range(1, 8):
        got(f"s{j}", stat.at[(t + 8 - j) % 8])
    total = stat[0]
    for j in range(1, 8):
        total = total + stat[j]
    inv_rms = lax.rsqrt(total[0:1] / OUT + 1e-05)
    weight_row = 2.0 / (OUT * cntr[0:1, :])
    row_loss = (inv_rms * inv_rms * total[1:2] - 2.0 * inv_rms * total[2:3] + total[3:4]) / OUT
    inner = weight_row * (inv_rms * total[1:2] - total[2:3])
    str_[...] = jnp.zeros_like(str_)
    str_[0:1, :] = inv_rms
    str_[1:2, :] = inv_rms * weight_row
    str_[2:3, :] = inv_rms * inv_rms * inv_rms * inner / OUT
    str_[3:4, :] = row_loss
    stc[...] = str_[...].T

    @pl.loop(0, LIVE // CHUNK)
    def _(i):
        rows = pl.ds(pl.multiple_of(i * CHUNK, CHUNK), CHUNK)
        there = pl.ds(pl.multiple_of(z * LIVE + i * CHUNK, CHUNK), CHUNK)
        joined = part[0, rows, :]
        stats = stc[rows, :]
        err = joined * stats[:, 0:1] * gain - wanted[rows, :].astype(F32)
        value = (stats[:, 1:2] * gain * err - joined * stats[:, 2:3]).astype(BF16)
        df[0, t, there, :] = value[:, 0:PART]
        df[1, t, there, :] = value[:, PART:BLOCK]

    def block(h, yy, zz, half=None):
        start, size = (0, LIVE) if half is None else (half * HALF, HALF)
        rows = pl.ds(pl.multiple_of((zz % 4) * LIVE + start, 16), size)
        return df.at[h, (yy % 4) * 2 + c, rows, :]

    def first(h, step, half=None):
        return block(0, y, z + step, half) if h == "z" else block(1, y + step, z, half)

    def second(h, b, step, half=None):
        if h == "z":
            return block(0, y + step, z + STEP[b], half)
        return block(1, y + STEP[b], z + step, half)

    def along(axis, step):
        return at(z=z + step) if axis == "z" else at(y=y + step)

    other = {"z": "y", "y": "z"}

    def put(name, ref, device):
        send(name, ref, ref, device)

    def spread_second(h, b):
        ref = second(h, b, 0)
        put(f"{h}2+{b}", ref, along(other[h], 1))
        put(f"{h}2-{b}", ref, along(other[h], 3))

    def pass_first(h):
        got(f"{h}1+", first(h, 3))
        put(f"{h}1f+", first(h, 3, 0), along(h, 1))
        got(f"{h}1-", first(h, 1))
        put(f"{h}1f-", first(h, 1, 1), along(h, 3))

    def end_first(h):
        got(f"{h}1f+", first(h, 2, 0))
        got(f"{h}1f-", first(h, 2, 1))

    def pass_second(h, b):
        got(f"{h}2+{b}", second(h, b, 3))
        put(f"{h}2f+{b}", second(h, b, 3, 0), along(other[h], 1))
        got(f"{h}2-{b}", second(h, b, 1))
        put(f"{h}2f-{b}", second(h, b, 1, 1), along(other[h], 3))

    def end_second(h, b):
        got(f"{h}2f+{b}", second(h, b, 2, 0))
        got(f"{h}2f-{b}", second(h, b, 2, 1))

    def whole(h, b, core):
        return df.at[h, ((y + STEP[b]) % 4) * 2 + core]

    def share(h, b):
        put(f"d{h}{b}", whole(h, b, c), sibling)

    def columns(h, b, o):
        core = c if o == 0 else 1 - c
        return (((y + STEP[b]) % 4) * 2 + core) * BLOCK + h * PART

    def grad(h, b, o):
        if o == 1:
            got(f"d{h}{b}", whole(h, b, 1 - c))
        cols = pl.ds(pl.multiple_of(columns(h, b, o), PART), PART)
        core = c if o == 0 else 1 - c
        gs[:, cols] = jnp.dot(
            xgt[...], df[h, ((y + STEP[b]) % 4) * 2 + core], preferred_element_type=F32
        ).astype(BF16)
        for j in (1, 2, 3):
            rows = pl.ds(pl.multiple_of(((x + j) % 4) * ROWS_OUT, 32), ROWS_OUT)
            send(f"g{h}{b}{o}{j}", gs.at[rows, cols], gr.at[j - 1, :, cols], at(x=x + j))

    def finish(h, b, o):
        column = columns(h, b, o)
        cols = pl.ds(pl.multiple_of(column, PART), PART)
        for j in (1, 2, 3):
            got(f"g{h}{b}{o}{j}", gr.at[j - 1, :, cols])
        largest = jnp.zeros((1, PART), F32)
        for l in range(3):
            mine = pl.ds(pl.multiple_of(x * ROWS_OUT + l * 32, 32), 32)
            there = pl.ds(pl.multiple_of(z * FEATS + l * 128 + x * 32, 32), 32)
            here = pl.ds(l * 32, 32)
            total = gs[mine, cols].astype(F32)
            for j in range(3):
                total = total + gr[j, here, cols].astype(F32)
            new = wv[there, cols].astype(F32) - learn_rate * total
            upd[here, cols] = new
            largest = jnp.maximum(largest, jnp.max(jnp.abs(new), axis=0, keepdims=True))
        for k in range(PART // 128):
            mx[pl.ds(column // 128 + k, 1), :] = largest[:, k * 128 : (k + 1) * 128]

    for h in "zy":
        put(f"{h}1+", first(h, 0), along(h, 1))
        put(f"{h}1-", first(h, 0), along(h, 3))
    for h in "zy":
        spread_second(h, 0)

    loss_rows = stc[0:LIVE, 3:4] * owner[...]
    request_loss = jnp.sum(loss_rows, axis=0, keepdims=True) / counts
    slots = slots_ref[...]
    places = slots // REQS * 8 + slots % REQS - d * 8
    hit = places == iota((REQS, REQS), 0)
    by_place = jnp.sum(jnp.where(hit, request_loss, 0.0), axis=1, keepdims=True)
    eye = iota((REQS, REQS), 0) == iota((REQS, REQS), 1)
    by_place = jnp.sum(jnp.where(eye, by_place, 0.0), axis=0, keepdims=True)
    dpr[pl.ds(d, 1), 32:40, :] = jnp.broadcast_to(by_place[None], (1, 8, 128))

    for h in "zy":
        pass_first(h)
        spread_second(h, 1)
        spread_second(h, 2)
    for h in "zy":
        end_first(h)
        spread_second(h, 3)
    share(0, 0)
    grad(0, 0, 0)
    pass_second("z", 0)
    pass_second("y", 0)
    grad(0, 0, 1)
    end_second("y", 0)
    share(1, 0)
    grad(1, 0, 0)
    pass_second("z", 1)
    pass_second("y", 1)
    grad(1, 0, 1)
    end_second("y", 1)
    share(1, 1)
    grad(1, 1, 0)
    pass_second("z", 2)
    pass_second("y", 2)
    grad(1, 1, 1)
    finish(0, 0, 0)
    finish(0, 0, 1)
    end_second("y", 2)
    share(1, 2)
    grad(1, 2, 0)
    finish(1, 0, 0)
    finish(1, 0, 1)
    pass_second("z", 3)
    share(0, 1)
    share(0, 2)
    pass_second("y", 3)
    grad(1, 2, 1)
    grad(0, 1, 0)
    grad(0, 2, 0)
    grad(0, 1, 1)
    grad(0, 2, 1)
    finish(1, 1, 0)
    finish(1, 1, 1)
    for b in range(4):
        end_second("z", b)
    share(0, 3)
    end_second("y", 3)
    share(1, 3)
    grad(0, 3, 0)
    grad(1, 3, 0)
    grad(0, 3, 1)
    grad(1, 3, 1)
    for h, b in ((1, 2), (0, 1), (0, 2), (0, 3), (1, 3)):
        finish(h, b, 0)
        finish(h, b, 1)

    for j in range(1, 8):
        send(f"m{j}", mx, mxr.at[j - 1], {"tp": (t + j) % 8, "dp": d})
    most = mx[...]
    for j in range(1, 8):
        got(f"m{j}", mxr.at[j - 1])
        most = jnp.maximum(most, mxr[j - 1])
    dpr[pl.ds(d, 1), 0:32, :] = most[None]
    for j in range(1, 16):
        send(f"n{j}", dpr.at[d], dpr.at[d], {"tp": t, "dp": (d + j) % 16})
    for j in range(1, 16):
        got(f"n{j}", dpr.at[(d + 16 - j) % 16])
    for j in range(16):
        most = jnp.maximum(most, dpr[j, 0:32, :])
        sprd[j * 8 : (j + 1) * 8, :] = dpr[j, 32:40, :]
    scale = most + 1e-06
    scale_ref[...] = scale
    for k in range(OUT // 128):
        cols = slice(k * 128, (k + 1) * 128)
        for l in range(3):
            serve_ref[l, :, cols] = (upd[l * 32 : (l + 1) * 32, cols] / scale[k : k + 1, :]).astype(BF16)
    lanes = iota((REQS, REQS), 1) == d * 8 + iota((REQS, REQS), 0) % 8
    mine = jnp.sum(jnp.where(lanes, sprd[...], 0.0), axis=1, keepdims=True)
    loss_ref[...] = jnp.sum(jnp.where(eye, mine, 0.0), axis=0, keepdims=True)
    for copy in sent:
        copy.wait_send()


def shards(hidden_rows, target_rows, row_counts, seq_slot, joining_weight, norm_gain):
    any_spec = pl.BlockSpec(memory_space=pl.ANY)
    vmem = pl.BlockSpec(memory_space=pltpu.VMEM)
    n = len(IDS)
    loss, serve, scale = pl.pallas_call(
        kernel,
        out_shape=(
            jax.ShapeDtypeStruct((1, REQS), F32),
            jax.ShapeDtypeStruct((3, 32, OUT), BF16),
            jax.ShapeDtypeStruct((32, 128), F32),
        ),
        in_specs=[any_spec, any_spec, vmem, vmem, any_spec, vmem],
        out_specs=(vmem, vmem, vmem),
        scratch_shapes=[
            pltpu.VMEM((3, SLOTS, BLOCK), BF16),
            pltpu.VMEM((SLOTS, BLOCK), BF16),
            pltpu.VMEM((4 * FEATS, OUT), BF16),
            pltpu.VMEM((LIVE, SLOTS), BF16),
            pltpu.VMEM((LIVE, 4 * FEATS), BF16),
            pltpu.VMEM((LIVE, BLOCK), BF16),
            pltpu.VMEM((4, LIVE, BLOCK), BF16),
            pltpu.VMEM((4, LIVE, BLOCK), BF16),
            pltpu.VMEM((3, LIVE, BLOCK), F32),
            pltpu.VMEM((2, HALF, BLOCK), BF16),
            pltpu.VMEM((2, LIVE, BLOCK), BF16),
            pltpu.VMEM((ALL, FEATS), BF16),
            pltpu.VMEM((FEATS, ALL), BF16),
            pltpu.VMEM((2, 8, ALL, PART), BF16),
            pltpu.VMEM((FEATS, OUT), BF16),
            pltpu.VMEM((3, ROWS_OUT, OUT), BF16),
            pltpu.VMEM((ROWS_OUT, OUT), F32),
            pltpu.VMEM((LIVE, REQS), F32),
            pltpu.VMEM((8, PAD), F32),
            pltpu.VMEM((PAD, 128), F32),
            pltpu.VMEM((128, PAD), F32),
            pltpu.VMEM((8, 8, PAD), F32),
            pltpu.VMEM((32, 128), F32),
            pltpu.VMEM((7, 32, 128), F32),
            pltpu.VMEM((16, 40, 128), F32),
            pltpu.VMEM((REQS, 128), F32),
            pltpu.SemaphoreType.DMA((15,)),
            pltpu.SemaphoreType.DMA((n,)),
            pltpu.SemaphoreType.DMA((n,)),
        ],
        compiler_params=pltpu.CompilerParams(
            collective_id=0, has_side_effects=True, vmem_limit_bytes=64 * 2**20 - 2**18
        ),
        name="joining_step",
    )(
        jnp.transpose(hidden_rows, (1, 0, 2)),
        target_rows,
        row_counts.reshape(1, REQS),
        seq_slot.reshape(1, REQS),
        joining_weight,
        norm_gain.reshape(8, BLOCK),
    )
    return loss.reshape(REQS), serve, scale.reshape(OUT)


def solution(mesh):
    placed = (P("dp", None, "tp"), P("dp", "tp"), P("dp"), P("dp"), P(None, "tp", None), P())
    return jax.shard_map(
        shards,
        mesh=mesh,
        in_specs=placed,
        out_specs=(P("dp"), P(None, ("tp", "dp"), None), P()),
        check_vma=False,
    )
```

profile of v0, /device:TPU:1, one launch (start us, length us, event | category | flops | bytes accessed | tf_op | source)
XLA Modules:
  0.0 142.7 jit_solution(16882628712727165827)
XLA Ops:
  0.6 1.3 reshape.23.gain_ref
  2.0 136.2 %joining_step.1 = (f32[1,128]{1,0:T(1,128)}, bf16[3,32,4096]{2,1,0:T(8,128)(2,1)}, f32[32,128]{1,0:T(8,128)}) custom-call(bf16[3,1024,512]{2,1,0:T(8,128)(2,1)} %bitcast.5, bf16[1024,512]{1,0:T(8,128)(2,1)} %tgt_hbm.1, s32[1,128]{1,0:T(1,128)} %bitcast.7, s32[1,128]{1,0:T(1,128)} %bitcast.8, bf16[3,512,4096]{2,1,0:T(8,128)(2,1)} %w_hbm.1, ...), custom_call_target="tpu_custom_call" | custom-call | tf_op jit(solution)/shard_map/joining_step/pallas_call | solution.py:452
  138.2 1.1 copy.12
  139.3 2.1 %copy.13 = bf16[3,32,4096]{2,1,0:T(8,128)(2,1)} copy(bf16[3,32,4096]{2,1,0:T(8,128)(2,1)} %get-tuple-element.13) | data formatting | bytes 1572864
  141.4 1.3 copy.14
where the time goes:
time: 143 us
  Pallas kernels  136 us (95%)
  local copies, waits for them, and re-layouts  5.84 us (4%)
    pallas_call x1, Pallas kernels, shards(): pl.pallas_call(kernel, out_shape=(jax.ShapeDtypeStruct((1, REQS), F32), j...  136 us
    unnamed x3, local copies, waits for them, and re-layouts  4.52 us

commit v1 on v0

v1 whole, which is shorter than its diff:
```python
import jax
import jax.numpy as jnp
from jax import lax
from jax.experimental import pallas as pl
from jax.experimental.pallas import tpu as pltpu
from jax.sharding import PartitionSpec as P

learn_rate = 1.0

F32, BF16, I32 = jnp.float32, jnp.bfloat16, jnp.int32
EXACT = lax.Precision.HIGHEST
REQS, MOST, SLOTS, LIVE = 128, 8, 1024, 544
HALF = LIVE // 2
PAD = 640
ALL = 4 * LIVE
BLOCK, PART = 512, 256
FEATS = 384
OUT = 4096
ROWS_OUT = 96
CHUNK = 32


def iota(shape, dim):
    return lax.broadcasted_iota(I32, shape, dim)


def names():
    out = [f"x{h}{j}" for h in range(2) for j in (1, 2, 3)] + [f"c{i}" for i in range(4)]
    out += ["h+", "h-", "f+a", "f+b", "f-a", "f-b"] + [f"s{j}" for j in range(1, 8)]
    for h in range(2):
        out += [f"{k}{h}{s}" for k in ("y", "yf") for s in "+-"]
        out += [f"{k}{h}{b}{s}" for k in ("a", "af") for b in range(4) for s in "+-"]
        out += [f"v{h}{j}" for j in (1, 2, 3)] + [f"d{h}{b}" for b in range(4)]
        out += [f"g{h}{b}{o}{j}" for b in range(4) for o in range(2) for j in (1, 2, 3)]
    out += [f"m{j}" for j in range(1, 8)] + [f"n{j}" for j in range(1, 16)]
    return {name: i for i, name in enumerate(out)}


IDS = names()
STEP = (0, 3, 1, 2)
ALONG = ((0, 2, 3), (0, 1, 3))
WHOLE = (1, 2)
TURN = (1, 3)


def kernel(
    hid_hbm, tgt_hbm, counts_ref, slots_ref, w_hbm, gain_ref,
    upd, small_ref,
    hid, tgt, wv, pick, perm, xc, xcb, wanted, crecv, part, hrecv, frecv, xg, xgt, df, gs, gr,
    owner, stc, str_, stat, mx, mxr, dpr, sprd, lsem, ss, rs,
):
    t = lax.axis_index("tp")
    d = lax.axis_index("dp")
    y, c = t // 2, t % 2
    z, x = d // 4, d % 4
    sent = []

    def at(y=y, c=c, z=z, x=x):
        return {"tp": (y % 4) * 2 + c, "dp": (z % 4) * 4 + x % 4}

    sibling = at(c=1 - c)

    def send(name, src, dst, device):
        i = IDS[name]
        copy = pltpu.make_async_remote_copy(
            src_ref=src, dst_ref=dst, send_sem=ss.at[i], recv_sem=rs.at[i],
            device_id=device, device_id_type=pl.DeviceIdType.MESH,
        )
        copy.start()
        sent.append(copy)

    def got(name, ref):
        i = IDS[name]
        pltpu.make_async_remote_copy(
            src_ref=ref, dst_ref=ref, send_sem=ss.at[i], recv_sem=rs.at[i],
            device_id=sibling, device_id_type=pl.DeviceIdType.MESH,
        ).wait_recv()

    loads = [pltpu.make_async_copy(hid_hbm.at[l], hid.at[l], lsem.at[l]) for l in range(3)]
    loads.append(pltpu.make_async_copy(tgt_hbm, tgt, lsem.at[3]))
    weights = []
    for zz in range(4):
        for l in range(3):
            weights.append(
                pltpu.make_async_copy(
                    w_hbm.at[l, pl.ds(zz * 128, 128)],
                    wv.at[pl.ds(zz * FEATS + l * 128, 128)],
                    lsem.at[4 + zz * 3 + l],
                )
            )
    for load in loads:
        load.start()
    barrier = pltpu.get_barrier_semaphore()
    for j in range(1, 8):
        pl.semaphore_signal(
            barrier, inc=1, device_id={"tp": (t + j) % 8, "dp": d}, device_id_type=pl.DeviceIdType.MESH
        )
    for j in range(1, 16):
        pl.semaphore_signal(
            barrier, inc=1, device_id={"tp": t, "dp": (d + j) % 16}, device_id_type=pl.DeviceIdType.MESH
        )

    counts = counts_ref[...].astype(F32)
    counts8 = jnp.broadcast_to(counts, (8, REQS))
    expand = (iota((REQS, SLOTS), 1) // MOST == iota((REQS, SLOTS), 0)).astype(F32)
    before = (iota((REQS, REQS), 0) < iota((REQS, REQS), 1)).astype(F32)
    start8 = jnp.dot(counts8, before, precision=EXACT, preferred_element_type=F32)
    count_slot = jnp.dot(counts8, expand, precision=EXACT, preferred_element_type=F32)
    start_slot = jnp.dot(start8, expand, precision=EXACT, preferred_element_type=F32)
    inside = iota((8, SLOTS), 1) % MOST
    rank8 = (start_slot + 0.5).astype(I32) + inside
    rank8 = jnp.where(inside < (count_slot + 0.5).astype(I32), rank8, -1)
    rank = rank8[0:1, :]

    @pl.loop(0, LIVE // 272)
    def _(i):
        rows = pl.ds(pl.multiple_of(i * 272, 16), 272)
        hit = iota((272, SLOTS), 0) + i * 272 == rank
        pick[rows, :] = jnp.where(hit, 1.0, 0.0).astype(BF16)

    place = iota((BLOCK, BLOCK), 1)
    source = place // 32 % 4 * 128 + place // 128 * 32 + place % 32
    perm[...] = (iota((BLOCK, BLOCK), 0) == source).astype(F32).astype(BF16)

    for load in loads:
        load.wait()
    for load in weights:
        load.start()

    @pl.loop(0, LIVE // 272)
    def _(i):
        rows = pl.ds(pl.multiple_of(i * 272, 16), 272)
        chosen = pick[rows, :]
        for l in range(3):
            got_rows = jnp.dot(chosen, hid[l], preferred_element_type=F32).astype(BF16)
            swapped = jnp.dot(got_rows, perm[...], preferred_element_type=F32).astype(BF16)
            for q in range(4):
                cols = slice(q * FEATS + l * 128, q * FEATS + (l + 1) * 128)
                xc[rows, cols] = got_rows[:, q * 128 : (q + 1) * 128]
                xcb[rows, cols] = swapped[:, q * 128 : (q + 1) * 128]

    pl.semaphore_wait(barrier, 22)

    def feats(q):
        return pl.ds(pl.multiple_of((q % 4) * FEATS, 128), FEATS)

    def rows_of(q):
        return pl.ds(pl.multiple_of((q % 4) * LIVE, 16), LIVE)

    me = (z, x)

    def axis(h, step):
        return at(z=z + step) if h == 0 else at(x=x + step)

    own_copies = []
    for h, kept in enumerate((xc, xcb)):
        for j in (1, 2, 3):
            send(f"x{h}{j}", kept.at[:, feats(me[h] + j)], xg.at[h, rows_of(me[h]), :], axis(h, j))
        own_copies.append(
            pltpu.make_async_copy(kept.at[:, feats(me[h])], xg.at[h, rows_of(me[h]), :], lsem.at[16 + h])
        )
        own_copies[h].start()

    turned_expand = (iota((SLOTS, REQS), 0) // MOST == iota((SLOTS, REQS), 1)).astype(F32).astype(BF16)

    @pl.loop(0, LIVE // 272)
    def _(i):
        rows = pl.ds(pl.multiple_of(i * 272, 16), 272)
        chosen = pick[rows, :]
        wanted[rows, :] = jnp.dot(chosen, tgt[...], preferred_element_type=F32).astype(BF16)
        owner[rows, :] = jnp.dot(chosen, turned_expand, preferred_element_type=F32)

    for load in weights:
        load.wait()

    def forward(yy, core, dst):
        column = ((yy % 4) * 2 + core) * BLOCK

        @pl.loop(0, 2)
        def _(i):
            cols = pl.ds(pl.multiple_of(column + i * PART, PART), PART)
            dst[:, pl.ds(pl.multiple_of(i * PART, PART), PART)] = jnp.dot(
                xc[...], wv[:, cols], preferred_element_type=F32
            ).astype(dst.dtype)

    csend = [pick.at[:, 0:BLOCK], pick.at[:, BLOCK : 2 * BLOCK], tgt.at[pl.ds(0, LIVE)], pick.at[:, 0:BLOCK]]

    def to_sibling(i, step):
        forward(y + step, 1 - c, csend[i])
        send(f"c{i}", csend[i], crecv.at[i], sibling)

    ysend = [hid.at[i, pl.ds(0, LIVE)] for i in range(3)]
    up, down = at(y=y + 1), at(y=y + 3)
    top, low = pl.ds(0, HALF), pl.ds(HALF, HALF)
    to_sibling(0, 2)
    first_sent = sent.pop()
    forward(y + 2, c, part.at[0])
    got("c0", crecv.at[0])
    ysend[0][...] = (part[0] + crecv[0].astype(F32)).astype(BF16)
    send("h+", ysend[0].at[top], hrecv.at[0], up)
    send("h-", ysend[0].at[low], hrecv.at[1], down)
    to_sibling(1, 1)
    forward(y + 1, c, part.at[1])
    got("c1", crecv.at[1])
    ysend[1][low, :] = (part[1, low, :] + crecv[1, low, :].astype(F32)).astype(BF16)
    send("f+a", ysend[1].at[low], frecv.at[0, low], up)
    to_sibling(2, 3)
    forward(y + 3, c, part.at[2])
    got("c2", crecv.at[2])
    ysend[2][top, :] = (part[2, top, :] + crecv[2, top, :].astype(F32)).astype(BF16)
    send("f-a", ysend[2].at[top], frecv.at[1, top], down)
    got("h+", hrecv.at[0])
    ysend[1][top, :] = (part[1, top, :] + crecv[1, top, :].astype(F32) + hrecv[0].astype(F32)).astype(BF16)
    send("f+b", ysend[1].at[top], frecv.at[0, top], up)
    got("h-", hrecv.at[1])
    ysend[2][low, :] = (part[2, low, :] + crecv[2, low, :].astype(F32) + hrecv[1].astype(F32)).astype(BF16)
    send("f-b", ysend[2].at[low], frecv.at[1, low], down)
    first_sent.wait_send()
    to_sibling(3, 0)
    forward(y, c, part.at[0])

    for h in range(2):
        own_copies[h].wait()
        for j in (1, 2, 3):
            got(f"x{h}{j}", xg.at[h, rows_of(me[h] + 4 - j), :])

        @pl.loop(0, ALL // 128)
        def _(k):
            places = pl.ds(pl.multiple_of(k * 128, 128), 128)
            turned = xg[h, places, :].T
            for q in range(4):
                for l in range(3):
                    xgt[h, q * ROWS_OUT + l * 32 : q * ROWS_OUT + (l + 1) * 32, places] = turned[
                        l * 128 + q * 32 : l * 128 + (q + 1) * 32, :
                    ]

    got("c3", crecv.at[3])
    got("f+a", frecv.at[0, low])
    got("f-a", frecv.at[1, top])
    got("f+b", frecv.at[0, top])
    got("f-b", frecv.at[1, low])
    gains = gain_ref[pl.ds(t * 4, 4), :]
    gain = jnp.concatenate([gains[k : k + 1, :] for k in range(4)], axis=1)
    stc[...] = jnp.zeros_like(stc)
    lane = iota((CHUNK, 128), 1)

    @pl.loop(0, LIVE // CHUNK)
    def _(i):
        rows = pl.ds(pl.multiple_of(i * CHUNK, CHUNK), CHUNK)
        joined = part[0, rows, :] + crecv[3, rows, :].astype(F32)
        joined = joined + (frecv[0, rows, :].astype(F32) + frecv[1, rows, :].astype(F32))
        part[0, rows, :] = joined
        goal = wanted[rows, :].astype(F32)
        scaled = joined * gain
        sums = [joined * joined, scaled * scaled, scaled * goal, goal * goal]
        row = jnp.zeros((CHUNK, 128), F32)
        for k, term in enumerate(sums):
            row = jnp.where(lane == k, jnp.sum(term, axis=1, keepdims=True), row)
        count = jnp.sum(owner[rows, :] * counts, axis=1, keepdims=True)
        stc[rows, :] = jnp.where(lane == 4, count, row)

    turned = stc[...].T
    count_row = jnp.maximum(turned[4:5, :], 1.0)
    stat[pl.ds(t, 1)] = turned[None, 0:8, :]
    for j in range(1, 8):
        send(f"s{j}", stat.at[t], stat.at[t], {"tp": (t + j) % 8, "dp": d})
    for j in range(1, 8):
        got(f"s{j}", stat.at[(t + 8 - j) % 8])
    total = stat[0]
    for j in range(1, 8):
        total = total + stat[j]
    inv_rms = lax.rsqrt(total[0:1] / OUT + 1e-05)
    weight_row = 2.0 / (OUT * count_row)
    row_loss = (inv_rms * inv_rms * total[1:2] - 2.0 * inv_rms * total[2:3] + total[3:4]) / OUT
    inner = weight_row * (inv_rms * total[1:2] - total[2:3])
    str_[...] = jnp.zeros_like(str_)
    str_[0:1, :] = inv_rms
    str_[1:2, :] = inv_rms * weight_row
    str_[2:3, :] = inv_rms * inv_rms * inv_rms * inner / OUT
    str_[3:4, :] = row_loss
    stc[...] = str_[...].T

    @pl.loop(0, LIVE // CHUNK)
    def _(i):
        rows = pl.ds(pl.multiple_of(i * CHUNK, CHUNK), CHUNK)
        joined = part[0, rows, :]
        stats = stc[rows, :]
        err = joined * stats[:, 0:1] * gain - wanted[rows, :].astype(F32)
        value = (stats[:, 1:2] * gain * err - joined * stats[:, 2:3]).astype(BF16)
        for h in range(2):
            there = pl.ds(pl.multiple_of(me[h] * LIVE + i * CHUNK, CHUNK), CHUNK)
            df[h, t, there, :] = value[:, h * PART : (h + 1) * PART]

    def block(h, yy, place, half=None):
        start, size = (0, LIVE) if half is None else (half * HALF, HALF)
        rows = pl.ds(pl.multiple_of((place % 4) * LIVE + start, 16), size)
        return df.at[h, (yy % 4) * 2 + c, rows, :]

    def put(name, ref, device):
        send(name, ref, ref, device)

    def put_y(h):
        put(f"y{h}+", block(h, y, me[h]), up)
        put(f"y{h}-", block(h, y, me[h]), down)

    def pass_y(h):
        got(f"y{h}+", block(h, y + 3, me[h]))
        put(f"yf{h}+", block(h, y + 3, me[h], 0), up)
        got(f"y{h}-", block(h, y + 1, me[h]))
        put(f"yf{h}-", block(h, y + 1, me[h], 1), down)

    def end_y(h):
        got(f"yf{h}+", block(h, y + 2, me[h], 0))
        got(f"yf{h}-", block(h, y + 2, me[h], 1))

    def put_axis(h, b):
        put(f"a{h}{b}+", block(h, y + STEP[b], me[h]), axis(h, 1))
        put(f"a{h}{b}-", block(h, y + STEP[b], me[h]), axis(h, 3))

    def pass_axis(h, b):
        got(f"a{h}{b}+", block(h, y + STEP[b], me[h] + 3))
        put(f"af{h}{b}+", block(h, y + STEP[b], me[h] + 3, 0), axis(h, 1))
        got(f"a{h}{b}-", block(h, y + STEP[b], me[h] + 1))
        put(f"af{h}{b}-", block(h, y + STEP[b], me[h] + 1, 1), axis(h, 3))

    def end_axis(h, b):
        got(f"af{h}{b}+", block(h, y + STEP[b], me[h] + 2, 0))
        got(f"af{h}{b}-", block(h, y + STEP[b], me[h] + 2, 1))

    def put_whole(h):
        for j in (1, 3, 2):
            put(f"v{h}{j}", block(h, y, me[h] + j), at(y=y + TURN[h]))

    def end_whole(h):
        for j in (1, 3, 2):
            got(f"v{h}{j}", block(h, y + 4 - TURN[h], me[h] + j))

    def whole(h, b, core):
        return df.at[h, ((y + STEP[b]) % 4) * 2 + core]

    def share(h, b):
        put(f"d{h}{b}", whole(h, b, c), sibling)

    def block_of(b, o):
        return ((y + STEP[b]) % 4) * 2 + (c if o == 0 else 1 - c)

    def across(h, step):
        return axis(1 - h, step)

    def grad(h, b, o):
        if o == 1:
            got(f"d{h}{b}", whole(h, b, 1 - c))
        cols = pl.ds(pl.multiple_of(block_of(b, o) * PART, PART), PART)
        gs[h, :, cols] = jnp.dot(xgt[h], df[h, block_of(b, o)], preferred_element_type=F32).astype(BF16)
        for j in (2, 1, 3):
            rows = pl.ds(pl.multiple_of(((me[1 - h] + j) % 4) * ROWS_OUT, 32), ROWS_OUT)
            send(f"g{h}{b}{o}{j}", gs.at[h, rows, cols], gr.at[h, j - 1, :, cols], across(h, j))

    def finish(h, b, o):
        column = block_of(b, o) * BLOCK + h * PART
        cols = pl.ds(pl.multiple_of(block_of(b, o) * PART, PART), PART)
        wide = pl.ds(pl.multiple_of(column, PART), PART)
        for j in (1, 2, 3):
            got(f"g{h}{b}{o}{j}", gr.at[h, j - 1, :, cols])
        largest = jnp.zeros((1, PART), F32)
        for l in range(3):
            mine = pl.ds(pl.multiple_of(me[1 - h] * ROWS_OUT + l * 32, 32), 32)
            there = pl.ds(pl.multiple_of(z * FEATS + l * 128 + x * 32, 32), 32)
            here = pl.ds(l * 32, 32)
            total = gs[h, mine, cols].astype(F32)
            for j in range(3):
                total = total + gr[h, j, here, cols].astype(F32)
            new = wv[there, wide].astype(F32) - learn_rate * total
            upd[l, :, wide] = new
            largest = jnp.maximum(largest, jnp.max(jnp.abs(new), axis=0, keepdims=True))
        for k in range(PART // 128):
            mx[pl.ds(column // 128 + k, 1), :] = largest[:, k * 128 : (k + 1) * 128]

    for h in range(2):
        put_y(h)
        put_axis(h, 0)

    loss_rows = stc[0:LIVE, 3:4] * owner[...]
    request_loss = jnp.sum(loss_rows, axis=0, keepdims=True) / counts
    slots = slots_ref[...]
    places = slots // REQS * 8 + slots % REQS - d * 8
    hit = places == iota((REQS, REQS), 0)
    by_place = jnp.sum(jnp.where(hit, request_loss, 0.0), axis=1, keepdims=True)
    eye = iota((REQS, REQS), 0) == iota((REQS, REQS), 1)
    by_place = jnp.sum(jnp.where(eye, by_place, 0.0), axis=0, keepdims=True)
    dpr[pl.ds(d, 1), 32:40, :] = jnp.broadcast_to(by_place[None], (1, 8, 128))

    for h in range(2):
        pass_axis(h, 0)
    for h in range(2):
        pass_y(h)
        put_axis(h, ALONG[h][1])
    for h in range(2):
        end_axis(h, 0)
        share(h, 0)
        put_whole(h)
    for h in range(2):
        grad(h, 0, 0)
    for h in range(2):
        end_y(h)
        put_axis(h, 3)
    for h in range(2):
        grad(h, 0, 1)
    for h in range(2):
        pass_axis(h, ALONG[h][1])
    for h in range(2):
        end_axis(h, ALONG[h][1])
        share(h, ALONG[h][1])
        grad(h, ALONG[h][1], 0)
    for h in range(2):
        grad(h, ALONG[h][1], 1)
    for h in range(2):
        pass_axis(h, 3)
    for h in range(2):
        finish(h, 0, 0)
        finish(h, 0, 1)
    for h in range(2):
        end_whole(h)
        share(h, WHOLE[h])
        grad(h, WHOLE[h], 0)
    for h in range(2):
        end_axis(h, 3)
        share(h, 3)
        grad(h, WHOLE[h], 1)
        grad(h, 3, 0)
    for h in range(2):
        grad(h, 3, 1)
    for h in range(2):
        for o in range(2):
            finish(h, ALONG[h][1], o)
    for h in range(2):
        for o in range(2):
            finish(h, WHOLE[h], o)
    for h in range(2):
        for o in range(2):
            finish(h, 3, o)

    for j in range(1, 8):
        send(f"m{j}", mx, mxr.at[j - 1], {"tp": (t + j) % 8, "dp": d})
    most = mx[...]
    for j in range(1, 8):
        got(f"m{j}", mxr.at[j - 1])
        most = jnp.maximum(most, mxr[j - 1])
    dpr[pl.ds(d, 1), 0:32, :] = most[None]
    for j in range(1, 16):
        send(f"n{j}", dpr.at[d], dpr.at[d], {"tp": t, "dp": (d + j) % 16})
    for j in range(1, 16):
        got(f"n{j}", dpr.at[(d + 16 - j) % 16])
    for j in range(16):
        most = jnp.maximum(most, dpr[j, 0:32, :])
        sprd[j * 8 : (j + 1) * 8, :] = dpr[j, 32:40, :]
    small_ref[0:32, :] = most + 1e-06
    lanes = iota((REQS, REQS), 1) == d * 8 + iota((REQS, REQS), 0) % 8
    mine = jnp.sum(jnp.where(lanes, sprd[...], 0.0), axis=1, keepdims=True)
    loss = jnp.sum(jnp.where(eye, mine, 0.0), axis=0, keepdims=True)
    small_ref[32:40, :] = jnp.broadcast_to(loss, (8, 128))
    for copy in sent:
        copy.wait_send()


def scaled(upd, small, loss_ref, serve_ref, scale_ref):
    scale_ref[...] = small[0:32, :]
    loss_ref[...] = small[32:33, :]
    for k in range(OUT // 128):
        cols = slice(k * 128, (k + 1) * 128)
        serve_ref[:, :, cols] = (upd[:, :, cols] / small[k : k + 1, :][None]).astype(BF16)


def shards(hidden_rows, target_rows, row_counts, seq_slot, joining_weight, norm_gain):
    any_spec = pl.BlockSpec(memory_space=pl.ANY)
    vmem = pl.BlockSpec(memory_space=pltpu.VMEM)
    n = len(IDS)
    upd, small = pl.pallas_call(
        kernel,
        out_shape=(
            jax.ShapeDtypeStruct((3, 32, OUT), F32),
            jax.ShapeDtypeStruct((40, 128), F32),
        ),
        in_specs=[any_spec, any_spec, vmem, vmem, any_spec, vmem],
        out_specs=(vmem, vmem),
        scratch_shapes=[
            pltpu.VMEM((3, SLOTS, BLOCK), BF16),
            pltpu.VMEM((SLOTS, BLOCK), BF16),
            pltpu.VMEM((4 * FEATS, OUT), BF16),
            pltpu.VMEM((LIVE, SLOTS), BF16),
            pltpu.VMEM((BLOCK, BLOCK), BF16),
            pltpu.VMEM((LIVE, 4 * FEATS), BF16),
            pltpu.VMEM((LIVE, 4 * FEATS), BF16),
            pltpu.VMEM((LIVE, BLOCK), BF16),
            pltpu.VMEM((4, LIVE, BLOCK), BF16),
            pltpu.VMEM((3, LIVE, BLOCK), F32),
            pltpu.VMEM((2, HALF, BLOCK), BF16),
            pltpu.VMEM((2, LIVE, BLOCK), BF16),
            pltpu.VMEM((2, ALL, FEATS), BF16),
            pltpu.VMEM((2, FEATS, ALL), BF16),
            pltpu.VMEM((2, 8, ALL, PART), BF16),
            pltpu.VMEM((2, FEATS, 8 * PART), BF16),
            pltpu.VMEM((2, 3, ROWS_OUT, 8 * PART), BF16),
            pltpu.VMEM((LIVE, REQS), F32),
            pltpu.VMEM((PAD, 128), F32),
            pltpu.VMEM((128, PAD), F32),
            pltpu.VMEM((8, 8, PAD), F32),
            pltpu.VMEM((32, 128), F32),
            pltpu.VMEM((7, 32, 128), F32),
            pltpu.VMEM((16, 40, 128), F32),
            pltpu.VMEM((REQS, 128), F32),
            pltpu.SemaphoreType.DMA((18,)),
            pltpu.SemaphoreType.DMA((n,)),
            pltpu.SemaphoreType.DMA((n,)),
        ],
        compiler_params=pltpu.CompilerParams(
            collective_id=0, has_side_effects=True, vmem_limit_bytes=64 * 2**20 - 2**18
        ),
        name="joining_step",
    )(
        jnp.transpose(hidden_rows, (1, 0, 2)),
        target_rows,
        row_counts.reshape(1, REQS),
        seq_slot.reshape(1, REQS),
        joining_weight,
        norm_gain.reshape(32, 128),
    )
    loss, serve, scale = pl.pallas_call(
        scaled,
        out_shape=(
            jax.ShapeDtypeStruct((1, REQS), F32),
            jax.ShapeDtypeStruct((3, 32, OUT), BF16),
            jax.ShapeDtypeStruct((32, 128), F32),
        ),
        in_specs=[vmem, vmem],
        out_specs=(vmem, vmem, vmem),
        name="scaled",
    )(upd, small)
    return loss.reshape(REQS), serve, scale.reshape(OUT)


def solution(mesh):
    placed = (P("dp", None, "tp"), P("dp", "tp"), P("dp"), P("dp"), P(None, "tp", None), P())
    return jax.shard_map(
        shards,
        mesh=mesh,
        in_specs=placed,
        out_specs=(P("dp"), P(None, ("tp", "dp"), None), P()),
        check_vma=False,
    )
```

time: 143 us -> 122 us (0.85)
  Pallas kernels: 136 us -> 122 us
  local copies, waits for them, and re-layouts: 5.84 us -> 0 us
    pallas_call x1 -> x2, Pallas kernels: 136 us -> 122 us  [the longest x1 119 us: shards(): pl.pallas_call(kernel, out_shape=(jax.ShapeDtypeStruct((3, 32, OUT), F32)...]
    unnamed x3 -> x0, local copies, waits for them, and re-layouts: 4.52 us -> none
where the time goes in v1:
time: 122 us
  Pallas kernels  122 us (100%)
    pallas_call x1, Pallas kernels, shards(): pl.pallas_call(kernel, out_shape=(jax.ShapeDtypeStruct((3, 32, OUT), F32)...  119 us
    pallas_call x1, Pallas kernels, shards(): pl.pallas_call(scaled, out_shape=(jax.ShapeDtypeStruct((1, REQS), F32), j...  2.47 us

profile of v1, /device:TPU:1, one launch (start us, length us, event | category | flops | bytes accessed | tf_op | source)
XLA Modules:
  0.0 122.2 jit_solution(8134050518539717348)
XLA Ops:
  0.6 119.1 %joining_step.1 = (f32[3,32,4096]{2,1,0:T(8,128)}, f32[40,128]{1,0:T(8,128)}) custom-call(bf16[3,1024,512]{2,1,0:T(8,128)(2,1)} %bitcast.6, bf16[1024,512]{1,0:T(8,128)(2,1)} %tgt_hbm.1, s32[1,128]{1,0:T(1,128)} %bitcast.8, s32[1,128]{1,0:T(1,128)} %bitcast.9, bf16[3,512,4096]{2,1,0:T(8,128)(2,1)} %w_hbm.1, f32[32,128]{1,0:T(8,128)} %bitcast.7), custom_call_target="tpu_custom_call" | custom-call | tf_op jit(solution)/shard_map/joining_step/pallas_call | solution.py:478
  119.7 2.5 %scaled.1 = (f32[1,128]{1,0:T(1,128)}, bf16[3,32,4096]{2,1,0:T(8,128)(2,1)}, f32[32,128]{1,0:T(8,128)}) custom-call(f32[3,32,4096]{2,1,0:T(8,128)} %get-tuple-element.8.upd, f32[40,128]{1,0:T(8,128)} %get-tuple-element.9.small), custom_call_target="tpu_custom_call" | custom-call | tf_op jit(solution)/shard_map/scaled/pallas_call | solution.py:528

commit v2 on v1

--- a/solution.py
+++ b/solution.py
@@ -26,11 +26,11 @@
 
 def names():
     out = [f"x{h}{j}" for h in range(2) for j in (1, 2, 3)] + [f"c{i}" for i in range(4)]
-    out += ["h+", "h-", "f+a", "f+b", "f-a", "f-b"] + [f"s{j}" for j in range(1, 8)]
+    out += ["c0b", "h+", "h-", "f+a", "f+b", "f-a", "f-b"] + [f"s{j}" for j in range(1, 8)]
     for h in range(2):
         out += [f"{k}{h}{s}" for k in ("y", "yf") for s in "+-"]
         out += [f"{k}{h}{b}{s}" for k in ("a", "af") for b in range(4) for s in "+-"]
-        out += [f"v{h}{j}" for j in (1, 2, 3)] + [f"d{h}{b}" for b in range(4)]
+        out += [f"v{h}{j}" for j in (1, 2, 3)] + [f"d{h}{b}{k}" for b in range(4) for k in range(4)]
         out += [f"g{h}{b}{o}{j}" for b in range(4) for o in range(2) for j in (1, 2, 3)]
     out += [f"m{j}" for j in range(1, 8)] + [f"n{j}" for j in range(1, 16)]
     return {name: i for i, name in enumerate(out)}
@@ -53,7 +53,7 @@
     d = lax.axis_index("dp")
     y, c = t // 2, t % 2
     z, x = d // 4, d % 4
-    sent = []
+    sent = {}
 
     def at(y=y, c=c, z=z, x=x):
         return {"tp": (y % 4) * 2 + c, "dp": (z % 4) * 4 + x % 4}
@@ -67,7 +67,11 @@
             device_id=device, device_id_type=pl.DeviceIdType.MESH,
         )
         copy.start()
-        sent.append(copy)
+        sent[name] = copy
+
+    def settle(*which):
+        for name in which or tuple(sent):
+            sent.pop(name).wait_send()
 
     def got(name, ref):
         i = IDS[name]
@@ -88,7 +92,7 @@
                     lsem.at[4 + zz * 3 + l],
                 )
             )
-    for load in loads:
+    for load in loads[:3]:
         load.start()
     barrier = pltpu.get_barrier_semaphore()
     for j in range(1, 8):
@@ -102,12 +106,12 @@
 
     counts = counts_ref[...].astype(F32)
     counts8 = jnp.broadcast_to(counts, (8, REQS))
-    expand = (iota((REQS, SLOTS), 1) // MOST == iota((REQS, SLOTS), 0)).astype(F32)
+    expand = (iota((REQS, SLOTS), 1) >> 3 == iota((REQS, SLOTS), 0)).astype(F32)
     before = (iota((REQS, REQS), 0) < iota((REQS, REQS), 1)).astype(F32)
     start8 = jnp.dot(counts8, before, precision=EXACT, preferred_element_type=F32)
     count_slot = jnp.dot(counts8, expand, precision=EXACT, preferred_element_type=F32)
     start_slot = jnp.dot(start8, expand, precision=EXACT, preferred_element_type=F32)
-    inside = iota((8, SLOTS), 1) % MOST
+    inside = iota((8, SLOTS), 1) & 7
     rank8 = (start_slot + 0.5).astype(I32) + inside
     rank8 = jnp.where(inside < (count_slot + 0.5).astype(I32), rank8, -1)
     rank = rank8[0:1, :]
@@ -118,12 +122,9 @@
         hit = iota((272, SLOTS), 0) + i * 272 == rank
         pick[rows, :] = jnp.where(hit, 1.0, 0.0).astype(BF16)
 
-    place = iota((BLOCK, BLOCK), 1)
-    source = place // 32 % 4 * 128 + place // 128 * 32 + place % 32
-    perm[...] = (iota((BLOCK, BLOCK), 0) == source).astype(F32).astype(BF16)
-
-    for load in loads:
+    for load in loads[:3]:
         load.wait()
+    loads[3].start()
     for load in weights:
         load.start()
 
@@ -133,11 +134,9 @@
         chosen = pick[rows, :]
         for l in range(3):
             got_rows = jnp.dot(chosen, hid[l], preferred_element_type=F32).astype(BF16)
-            swapped = jnp.dot(got_rows, perm[...], preferred_element_type=F32).astype(BF16)
             for q in range(4):
                 cols = slice(q * FEATS + l * 128, q * FEATS + (l + 1) * 128)
                 xc[rows, cols] = got_rows[:, q * 128 : (q + 1) * 128]
-                xcb[rows, cols] = swapped[:, q * 128 : (q + 1) * 128]
 
     pl.semaphore_wait(barrier, 22)
 
@@ -153,7 +152,8 @@
         return at(z=z + step) if h == 0 else at(x=x + step)
 
     own_copies = []
-    for h, kept in enumerate((xc, xcb)):
+
+    def exchange(h, kept):
         for j in (1, 2, 3):
             send(f"x{h}{j}", kept.at[:, feats(me[h] + j)], xg.at[h, rows_of(me[h]), :], axis(h, j))
         own_copies.append(
@@ -161,7 +161,77 @@
         )
         own_copies[h].start()
 
-    turned_expand = (iota((SLOTS, REQS), 0) // MOST == iota((SLOTS, REQS), 1)).astype(F32).astype(BF16)
+    exchange(0, xc)
+    for load in weights:
+        load.wait()
+
+    def forward(yy, core, dst, rows=slice(None)):
+        column = ((yy % 4) * 2 + core) * BLOCK
+
+        @pl.loop(0, 2)
+        def _(i):
+            cols = pl.ds(pl.multiple_of(column + i * PART, PART), PART)
+            dst[rows, pl.ds(pl.multiple_of(i * PART, PART), PART)] = jnp.dot(
+                xc[rows, :], wv[:, cols], preferred_element_type=F32
+            ).astype(dst.dtype)
+
+    csend = [xcb.at[:, i * BLOCK : (i + 1) * BLOCK] for i in range(3)] + [hid.at[2, pl.ds(0, LIVE)]]
+    ysend = [hid.at[i, pl.ds(0, LIVE)] for i in range(2)]
+    yhalf = [hid.at[i, pl.ds(LIVE, HALF)] for i in range(2)]
+
+    def to_sibling(i, step):
+        forward(y + step, 1 - c, csend[i])
+        send(f"c{i}", csend[i], crecv.at[i], sibling)
+
+    up, down = at(y=y + 1), at(y=y + 3)
+    top, low = pl.ds(0, HALF), pl.ds(HALF, HALF)
+    for rows, name in ((top, "c0"), (low, "c0b")):
+        forward(y + 2, 1 - c, csend[0], rows)
+        send(name, csend[0].at[rows], crecv.at[0, rows], sibling)
+        forward(y + 2, c, part.at[0], rows)
+    for k, (rows, name, there, device) in enumerate(((top, "c0", "h+", up), (low, "c0b", "h-", down))):
+        got(name, crecv.at[0, rows])
+        yhalf[k][...] = (part[0, rows, :] + crecv[0, rows, :].astype(F32)).astype(BF16)
+        send(there, yhalf[k], hrecv.at[k], device)
+    to_sibling(1, 1)
+    forward(y + 1, c, part.at[1])
+    got("c1", crecv.at[1])
+    ysend[0][low, :] = (part[1, low, :] + crecv[1, low, :].astype(F32)).astype(BF16)
+    send("f+a", ysend[0].at[low], frecv.at[0, low], up)
+    to_sibling(2, 3)
+    forward(y + 3, c, part.at[2])
+    got("c2", crecv.at[2])
+    ysend[1][top, :] = (part[2, top, :] + crecv[2, top, :].astype(F32)).astype(BF16)
+    send("f-a", ysend[1].at[top], frecv.at[1, top], down)
+
+    place = iota((BLOCK, BLOCK), 1)
+    source = ((place >> 5) & 3) * 128 + (place >> 7) * 32 + (place & 31)
+    perm[...] = (iota((BLOCK, BLOCK), 0) == source).astype(F32).astype(BF16)
+
+    settle("c0", "c0b", "c1", "c2")
+
+    @pl.loop(0, LIVE // 272)
+    def _(i):
+        rows = pl.ds(pl.multiple_of(i * 272, 16), 272)
+        for l in range(3):
+            whole_rows = jnp.concatenate(
+                [xc[rows, q * FEATS + l * 128 : q * FEATS + (l + 1) * 128] for q in range(4)], axis=1
+            )
+            swapped = jnp.dot(whole_rows, perm[...], preferred_element_type=F32).astype(BF16)
+            for q in range(4):
+                xcb[rows, q * FEATS + l * 128 : q * FEATS + (l + 1) * 128] = swapped[:, q * 128 : (q + 1) * 128]
+
+    exchange(1, xcb)
+    got("h+", hrecv.at[0])
+    ysend[0][top, :] = (part[1, top, :] + crecv[1, top, :].astype(F32) + hrecv[0].astype(F32)).astype(BF16)
+    send("f+b", ysend[0].at[top], frecv.at[0, top], up)
+    got("h-", hrecv.at[1])
+    ysend[1][low, :] = (part[2, low, :] + crecv[2, low, :].astype(F32) + hrecv[1].astype(F32)).astype(BF16)
+    send("f-b", ysend[1].at[low], frecv.at[1, low], down)
+    to_sibling(3, 0)
+    forward(y, c, part.at[0])
+    turned_expand = (iota((SLOTS, REQS), 0) >> 3 == iota((SLOTS, REQS), 1)).astype(F32).astype(BF16)
+    loads[3].wait()
 
     @pl.loop(0, LIVE // 272)
     def _(i):
@@ -170,54 +240,6 @@
         wanted[rows, :] = jnp.dot(chosen, tgt[...], preferred_element_type=F32).astype(BF16)
         owner[rows, :] = jnp.dot(chosen, turned_expand, preferred_element_type=F32)
 
-    for load in weights:
-        load.wait()
-
-    def forward(yy, core, dst):
-        column = ((yy % 4) * 2 + core) * BLOCK
-
-        @pl.loop(0, 2)
-        def _(i):
-            cols = pl.ds(pl.multiple_of(column + i * PART, PART), PART)
-            dst[:, pl.ds(pl.multiple_of(i * PART, PART), PART)] = jnp.dot(
-                xc[...], wv[:, cols], preferred_element_type=F32
-            ).astype(dst.dtype)
-
-    csend = [pick.at[:, 0:BLOCK], pick.at[:, BLOCK : 2 * BLOCK], tgt.at[pl.ds(0, LIVE)], pick.at[:, 0:BLOCK]]
-
-    def to_sibling(i, step):
-        forward(y + step, 1 - c, csend[i])
-        send(f"c{i}", csend[i], crecv.at[i], sibling)
-
-    ysend = [hid.at[i, pl.ds(0, LIVE)] for i in range(3)]
-    up, down = at(y=y + 1), at(y=y + 3)
-    top, low = pl.ds(0, HALF), pl.ds(HALF, HALF)
-    to_sibling(0, 2)
-    first_sent = sent.pop()
-    forward(y + 2, c, part.at[0])
-    got("c0", crecv.at[0])
-    ysend[0][...] = (part[0] + crecv[0].astype(F32)).astype(BF16)
-    send("h+", ysend[0].at[top], hrecv.at[0], up)
-    send("h-", ysend[0].at[low], hrecv.at[1], down)
-    to_sibling(1, 1)
-    forward(y + 1, c, part.at[1])
-    got("c1", crecv.at[1])
-    ysend[1][low, :] = (part[1, low, :] + crecv[1, low, :].astype(F32)).astype(BF16)
-    send("f+a", ysend[1].at[low], frecv.at[0, low], up)
-    to_sibling(2, 3)
-    forward(y + 3, c, part.at[2])
-    got("c2", crecv.at[2])
-    ysend[2][top, :] = (part[2, top, :] + crecv[2, top, :].astype(F32)).astype(BF16)
-    send("f-a", ysend[2].at[top], frecv.at[1, top], down)
-    got("h+", hrecv.at[0])
-    ysend[1][top, :] = (part[1, top, :] + crecv[1, top, :].astype(F32) + hrecv[0].astype(F32)).astype(BF16)
-    send("f+b", ysend[1].at[top], frecv.at[0, top], up)
-    got("h-", hrecv.at[1])
-    ysend[2][low, :] = (part[2, low, :] + crecv[2, low, :].astype(F32) + hrecv[1].astype(F32)).astype(BF16)
-    send("f-b", ysend[2].at[low], frecv.at[1, low], down)
-    first_sent.wait_send()
-    to_sibling(3, 0)
-    forward(y, c, part.at[0])
 
     for h in range(2):
         own_copies[h].wait()
@@ -323,9 +345,12 @@
         got(f"a{h}{b}-", block(h, y + STEP[b], me[h] + 1))
         put(f"af{h}{b}-", block(h, y + STEP[b], me[h] + 1, 1), axis(h, 3))
 
+        share(h, b, 0, 1, 3)
+
     def end_axis(h, b):
         got(f"af{h}{b}+", block(h, y + STEP[b], me[h] + 2, 0))
         got(f"af{h}{b}-", block(h, y + STEP[b], me[h] + 2, 1))
+        share(h, b, 2)
 
     def put_whole(h):
         for j in (1, 3, 2):
@@ -334,12 +359,16 @@
     def end_whole(h):
         for j in (1, 3, 2):
             got(f"v{h}{j}", block(h, y + 4 - TURN[h], me[h] + j))
-
-    def whole(h, b, core):
-        return df.at[h, ((y + STEP[b]) % 4) * 2 + core]
-
-    def share(h, b):
-        put(f"d{h}{b}", whole(h, b, c), sibling)
+            share(h, WHOLE[h], j)
+
+    def share(h, b, *steps):
+        for k in steps:
+            put(f"d{h}{b}{k}", block(h, y + STEP[b], me[h] + k), sibling)
+
+    def shared(h, b):
+        for k in range(4):
+            rows = rows_of(me[h] + k)
+            got(f"d{h}{b}{k}", df.at[h, block_of(b, 1), rows, :])
 
     def block_of(b, o):
         return ((y + STEP[b]) % 4) * 2 + (c if o == 0 else 1 - c)
@@ -349,7 +378,7 @@
 
     def grad(h, b, o):
         if o == 1:
-            got(f"d{h}{b}", whole(h, b, 1 - c))
+            shared(h, b)
         cols = pl.ds(pl.multiple_of(block_of(b, o) * PART, PART), PART)
         gs[h, :, cols] = jnp.dot(xgt[h], df[h, block_of(b, o)], preferred_element_type=F32).astype(BF16)
         for j in (2, 1, 3):
@@ -376,6 +405,7 @@
         for k in range(PART // 128):
             mx[pl.ds(column // 128 + k, 1), :] = largest[:, k * 128 : (k + 1) * 128]
 
+    early = tuple(sent)
     for h in range(2):
         put_y(h)
         put_axis(h, 0)
@@ -383,13 +413,14 @@
     loss_rows = stc[0:LIVE, 3:4] * owner[...]
     request_loss = jnp.sum(loss_rows, axis=0, keepdims=True) / counts
     slots = slots_ref[...]
-    places = slots // REQS * 8 + slots % REQS - d * 8
+    places = (slots >> 7) * 8 + (slots & 127) - d * 8
     hit = places == iota((REQS, REQS), 0)
     by_place = jnp.sum(jnp.where(hit, request_loss, 0.0), axis=1, keepdims=True)
     eye = iota((REQS, REQS), 0) == iota((REQS, REQS), 1)
     by_place = jnp.sum(jnp.where(eye, by_place, 0.0), axis=0, keepdims=True)
     dpr[pl.ds(d, 1), 32:40, :] = jnp.broadcast_to(by_place[None], (1, 8, 128))
 
+    settle(*early)
     for h in range(2):
         pass_axis(h, 0)
     for h in range(2):
@@ -397,20 +428,18 @@
         put_axis(h, ALONG[h][1])
     for h in range(2):
         end_axis(h, 0)
-        share(h, 0)
-        put_whole(h)
-    for h in range(2):
         grad(h, 0, 0)
     for h in range(2):
         end_y(h)
         put_axis(h, 3)
-    for h in range(2):
+        put_whole(h)
+    for h in range(2):
+        share(h, WHOLE[h], 0)
         grad(h, 0, 1)
     for h in range(2):
         pass_axis(h, ALONG[h][1])
     for h in range(2):
         end_axis(h, ALONG[h][1])
-        share(h, ALONG[h][1])
         grad(h, ALONG[h][1], 0)
     for h in range(2):
         grad(h, ALONG[h][1], 1)
@@ -420,13 +449,7 @@
         finish(h, 0, 0)
         finish(h, 0, 1)
     for h in range(2):
-        end_whole(h)
-        share(h, WHOLE[h])
-        grad(h, WHOLE[h], 0)
-    for h in range(2):
         end_axis(h, 3)
-        share(h, 3)
-        grad(h, WHOLE[h], 1)
         grad(h, 3, 0)
     for h in range(2):
         grad(h, 3, 1)
@@ -434,14 +457,21 @@
         for o in range(2):
             finish(h, ALONG[h][1], o)
     for h in range(2):
+        end_whole(h)
+        grad(h, WHOLE[h], 0)
+    for h in range(2):
+        grad(h, WHOLE[h], 1)
+    settle(*(name for name in tuple(sent) if name[0] != "g"))
+    for h in range(2):
+        for o in range(2):
+            finish(h, 3, o)
+    for h in range(2):
         for o in range(2):
             finish(h, WHOLE[h], o)
-    for h in range(2):
-        for o in range(2):
-            finish(h, 3, o)
 
     for j in range(1, 8):
         send(f"m{j}", mx, mxr.at[j - 1], {"tp": (t + j) % 8, "dp": d})
+    settle(*(name for name in tuple(sent) if name[0] == "g"))
     most = mx[...]
     for j in range(1, 8):
         got(f"m{j}", mxr.at[j - 1])
@@ -455,12 +485,11 @@
         most = jnp.maximum(most, dpr[j, 0:32, :])
         sprd[j * 8 : (j + 1) * 8, :] = dpr[j, 32:40, :]
     small_ref[0:32, :] = most + 1e-06
-    lanes = iota((REQS, REQS), 1) == d * 8 + iota((REQS, REQS), 0) % 8
+    lanes = iota((REQS, REQS), 1) == d * 8 + (iota((REQS, REQS), 0) & 7)
     mine = jnp.sum(jnp.where(lanes, sprd[...], 0.0), axis=1, keepdims=True)
     loss = jnp.sum(jnp.where(eye, mine, 0.0), axis=0, keepdims=True)
     small_ref[32:40, :] = jnp.broadcast_to(loss, (8, 128))
-    for copy in sent:
-        copy.wait_send()
+    settle()
 
 
 def scaled(upd, small, loss_ref, serve_ref, scale_ref):

time: 122 us -> 133 us (1.090)
  Pallas kernels: 122 us -> 132 us
    pallas_call x1, Pallas kernels: 119 us -> 129 us  [shards(): pl.pallas_call(kernel, out_shape=(jax.ShapeDtypeStruct((3, 32, OUT), F32)...]
where the time goes in v2:
time: 133 us; the launch traced here: 132 us
  Pallas kernels  132 us (99%)
    pallas_call x1, Pallas kernels, shards(): pl.pallas_call(kernel, out_shape=(jax.ShapeDtypeStruct((3, 32, OUT), F32)...  129 us

profile of v2, /device:TPU:1, one launch (start us, length us, event | category | flops | bytes accessed | tf_op | source)
XLA Modules:
  0.0 132.3 jit_solution(7691759898258495372)
XLA Ops:
  0.6 129.2 %joining_step.1 = (f32[3,32,4096]{2,1,0:T(8,128)}, f32[40,128]{1,0:T(8,128)}) custom-call(bf16[3,1024,512]{2,1,0:T(8,128)(2,1)} %bitcast.6, bf16[1024,512]{1,0:T(8,128)(2,1)} %tgt_hbm.1, s32[1,128]{1,0:T(1,128)} %bitcast.8, s32[1,128]{1,0:T(1,128)} %bitcast.9, bf16[3,512,4096]{2,1,0:T(8,128)(2,1)} %w_hbm.1, f32[32,128]{1,0:T(8,128)} %bitcast.7), custom_call_target="tpu_custom_call" | custom-call | tf_op jit(solution)/shard_map/joining_step/pallas_call | solution.py:507
  129.8 2.5 %scaled.1 = (f32[1,128]{1,0:T(1,128)}, bf16[3,32,4096]{2,1,0:T(8,128)(2,1)}, f32[32,128]{1,0:T(8,128)}) custom-call(f32[3,32,4096]{2,1,0:T(8,128)} %get-tuple-element.8.upd, f32[40,128]{1,0:T(8,128)} %get-tuple-element.9.small), custom_call_target="tpu_custom_call" | custom-call | tf_op jit(solution)/shard_map/scaled/pallas_call | solution.py:557

commit v3 on v2

--- a/solution.py
+++ b/solution.py
@@ -28,7 +28,7 @@
     out = [f"x{h}{j}" for h in range(2) for j in (1, 2, 3)] + [f"c{i}" for i in range(4)]
     out += ["c0b", "h+", "h-", "f+a", "f+b", "f-a", "f-b"] + [f"s{j}" for j in range(1, 8)]
     for h in range(2):
-        out += [f"{k}{h}{s}" for k in ("y", "yf") for s in "+-"]
+        out += [f"{k}{h}{s}" for k in ("y", "yf", "e") for s in "+-"]
         out += [f"{k}{h}{b}{s}" for k in ("a", "af") for b in range(4) for s in "+-"]
         out += [f"v{h}{j}" for j in (1, 2, 3)] + [f"d{h}{b}{k}" for b in range(4) for k in range(4)]
         out += [f"g{h}{b}{o}{j}" for b in range(4) for o in range(2) for j in (1, 2, 3)]
@@ -241,21 +241,6 @@
         owner[rows, :] = jnp.dot(chosen, turned_expand, preferred_element_type=F32)
 
 
-    for h in range(2):
-        own_copies[h].wait()
-        for j in (1, 2, 3):
-            got(f"x{h}{j}", xg.at[h, rows_of(me[h] + 4 - j), :])
-
-        @pl.loop(0, ALL // 128)
-        def _(k):
-            places = pl.ds(pl.multiple_of(k * 128, 128), 128)
-            turned = xg[h, places, :].T
-            for q in range(4):
-                for l in range(3):
-                    xgt[h, q * ROWS_OUT + l * 32 : q * ROWS_OUT + (l + 1) * 32, places] = turned[
-                        l * 128 + q * 32 : l * 128 + (q + 1) * 32, :
-                    ]
-
     got("c3", crecv.at[3])
     got("f+a", frecv.at[0, low])
     got("f-a", frecv.at[1, top])
@@ -321,19 +306,47 @@
     def put(name, ref, device):
         send(name, ref, ref, device)
 
-    def put_y(h):
-        put(f"y{h}+", block(h, y, me[h]), up)
-        put(f"y{h}-", block(h, y, me[h]), down)
-
-    def pass_y(h):
-        got(f"y{h}+", block(h, y + 3, me[h]))
-        put(f"yf{h}+", block(h, y + 3, me[h], 0), up)
-        got(f"y{h}-", block(h, y + 1, me[h]))
-        put(f"yf{h}-", block(h, y + 1, me[h], 1), down)
-
-    def end_y(h):
-        got(f"yf{h}+", block(h, y + 2, me[h], 0))
-        got(f"yf{h}-", block(h, y + 2, me[h], 1))
+    up_first = (False, True)
+    early_half = (1, 0)
+
+    def put_y(h, second):
+        if up_first[h] != second:
+            put(f"y{h}+", block(h, y, me[h]), up)
+        else:
+            put(f"y{h}-", block(h, y, me[h]), down)
+
+    def pass_y(h, second):
+        if up_first[h] != second:
+            got(f"y{h}+", block(h, y + 3, me[h]))
+            put(f"yf{h}+", block(h, y + 3, me[h], 0), up)
+        else:
+            got(f"y{h}-", block(h, y + 1, me[h]))
+            put(f"yf{h}-", block(h, y + 1, me[h], 1), down)
+
+    def end_y(h, half):
+        got(f"yf{h}" + "+-"[half], block(h, y + 2, me[h], half))
+
+    def put_far(h, half):
+        name = "e" if half == early_half[h] else "a"
+        last = "" if name == "e" else "3"
+        put(f"{name}{h}{last}+", block(h, y + 2, me[h], half), axis(h, 1))
+        put(f"{name}{h}{last}-", block(h, y + 2, me[h], half), axis(h, 3))
+
+    def pass_far(h):
+        half = early_half[h]
+        got(f"e{h}+", block(h, y + 2, me[h] + 3, half))
+        put(f"af{h}3+", block(h, y + 2, me[h] + 3, half), axis(h, 1))
+        got(f"e{h}-", block(h, y + 2, me[h] + 1, half))
+        half = 1 - half
+        got(f"a{h}3-", block(h, y + 2, me[h] + 1, half))
+        put(f"af{h}3-", block(h, y + 2, me[h] + 1, half), axis(h, 3))
+        got(f"a{h}3+", block(h, y + 2, me[h] + 3, half))
+        share(h, 3, 0, 1, 3)
+
+    def end_far(h):
+        got(f"af{h}3+", block(h, y + 2, me[h] + 2, early_half[h]))
+        got(f"af{h}3-", block(h, y + 2, me[h] + 2, 1 - early_half[h]))
+        share(h, 3, 2)
 
     def put_axis(h, b):
         put(f"a{h}{b}+", block(h, y + STEP[b], me[h]), axis(h, 1))
@@ -352,8 +365,8 @@
         got(f"af{h}{b}-", block(h, y + STEP[b], me[h] + 2, 1))
         share(h, b, 2)
 
-    def put_whole(h):
-        for j in (1, 3, 2):
+    def put_whole(h, *steps):
+        for j in steps:
             put(f"v{h}{j}", block(h, y, me[h] + j), at(y=y + TURN[h]))
 
     def end_whole(h):
@@ -407,7 +420,7 @@
 
     early = tuple(sent)
     for h in range(2):
-        put_y(h)
+        put_y(h, False)
         put_axis(h, 0)
 
     loss_rows = stc[0:LIVE, 3:4] * owner[...]
@@ -422,34 +435,57 @@
 
     settle(*early)
     for h in range(2):
+        own_copies[h].wait()
+        for j in (1, 2, 3):
+            got(f"x{h}{j}", xg.at[h, rows_of(me[h] + 4 - j), :])
+
+        @pl.loop(0, ALL // 128)
+        def _(k):
+            places = pl.ds(pl.multiple_of(k * 128, 128), 128)
+            turned = xg[h, places, :].T
+            for q in range(4):
+                for l in range(3):
+                    xgt[h, q * ROWS_OUT + l * 32 : q * ROWS_OUT + (l + 1) * 32, places] = turned[
+                        l * 128 + q * 32 : l * 128 + (q + 1) * 32, :
+                    ]
+
+    for h in range(2):
         pass_axis(h, 0)
     for h in range(2):
-        pass_y(h)
+        pass_y(h, False)
         put_axis(h, ALONG[h][1])
+    for h in range(2):
+        put_y(h, True)
     for h in range(2):
         end_axis(h, 0)
         grad(h, 0, 0)
     for h in range(2):
-        end_y(h)
-        put_axis(h, 3)
-        put_whole(h)
-    for h in range(2):
+        end_y(h, early_half[h])
+        put_far(h, early_half[h])
+    for h in range(2):
+        pass_y(h, True)
+        put_whole(h, 1)
         share(h, WHOLE[h], 0)
+    for h in range(2):
         grad(h, 0, 1)
     for h in range(2):
         pass_axis(h, ALONG[h][1])
+    for h in range(2):
+        end_y(h, 1 - early_half[h])
+        put_far(h, 1 - early_half[h])
+        put_whole(h, 3, 2)
     for h in range(2):
         end_axis(h, ALONG[h][1])
         grad(h, ALONG[h][1], 0)
     for h in range(2):
         grad(h, ALONG[h][1], 1)
     for h in range(2):
-        pass_axis(h, 3)
+        pass_far(h)
     for h in range(2):
         finish(h, 0, 0)
         finish(h, 0, 1)
     for h in range(2):
-        end_axis(h, 3)
+        end_far(h)
         grad(h, 3, 0)
     for h in range(2):
         grad(h, 3, 1)

time: 133 us -> 118 us (0.89)
  Pallas kernels: 132 us -> 117 us
    pallas_call x1, Pallas kernels: 129 us -> 115 us  [shards(): pl.pallas_call(kernel, out_shape=(jax.ShapeDtypeStruct((3, 32, OUT), F32)...]
where the time goes in v3:
time: 118 us
  Pallas kernels  117 us (99%)
    pallas_call x1, Pallas kernels, shards(): pl.pallas_call(kernel, out_shape=(jax.ShapeDtypeStruct((3, 32, OUT), F32)...  115 us
    pallas_call x1, Pallas kernels, shards(): pl.pallas_call(scaled, out_shape=(jax.ShapeDtypeStruct((1, REQS), F32), j...  2.47 us

profile of v3, /device:TPU:1, one launch (start us, length us, event | category | flops | bytes accessed | tf_op | source)
XLA Modules:
  0.0 117.9 jit_solution(13264358643640885721)
XLA Ops:
  0.6 114.8 %joining_step.1 = (f32[3,32,4096]{2,1,0:T(8,128)}, f32[40,128]{1,0:T(8,128)}) custom-call(bf16[3,1024,512]{2,1,0:T(8,128)(2,1)} %bitcast.6, bf16[1024,512]{1,0:T(8,128)(2,1)} %tgt_hbm.1, s32[1,128]{1,0:T(1,128)} %bitcast.8, s32[1,128]{1,0:T(1,128)} %bitcast.9, bf16[3,512,4096]{2,1,0:T(8,128)(2,1)} %w_hbm.1, f32[32,128]{1,0:T(8,128)} %bitcast.7), custom_call_target="tpu_custom_call" | custom-call | tf_op jit(solution)/shard_map/joining_step/pallas_call | solution.py:543
  115.5 2.5 %scaled.1 = (f32[1,128]{1,0:T(1,128)}, bf16[3,32,4096]{2,1,0:T(8,128)(2,1)}, f32[32,128]{1,0:T(8,128)}) custom-call(f32[3,32,4096]{2,1,0:T(8,128)} %get-tuple-element.8.upd, f32[40,128]{1,0:T(8,128)} %get-tuple-element.9.small), custom_call_target="tpu_custom_call" | custom-call | tf_op jit(solution)/shard_map/scaled/pallas_call | solution.py:593

commit v4 on v3

--- a/solution.py
+++ b/solution.py
@@ -32,7 +32,7 @@
         out += [f"{k}{h}{b}{s}" for k in ("a", "af") for b in range(4) for s in "+-"]
         out += [f"v{h}{j}" for j in (1, 2, 3)] + [f"d{h}{b}{k}" for b in range(4) for k in range(4)]
         out += [f"g{h}{b}{o}{j}" for b in range(4) for o in range(2) for j in (1, 2, 3)]
-    out += [f"m{j}" for j in range(1, 8)] + [f"n{j}" for j in range(1, 16)]
+    out += [f"m{j}" for j in range(1, 8)] + [f"{k}{j}" for k in "no" for j in range(1, 16)]
     return {name: i for i, name in enumerate(out)}
 
 
@@ -47,7 +47,7 @@
     hid_hbm, tgt_hbm, counts_ref, slots_ref, w_hbm, gain_ref,
     upd, small_ref,
     hid, tgt, wv, pick, perm, xc, xcb, wanted, crecv, part, hrecv, frecv, xg, xgt, df, gs, gr,
-    owner, stc, str_, stat, mx, mxr, dpr, sprd, lsem, ss, rs,
+    owner, stc, str_, stat, mxp, mx, mxr, dpr, dpl, sprd, lsem, ss, rs,
 ):
     t = lax.axis_index("tp")
     d = lax.axis_index("dp")
@@ -175,7 +175,7 @@
                 xc[rows, :], wv[:, cols], preferred_element_type=F32
             ).astype(dst.dtype)
 
-    csend = [xcb.at[:, i * BLOCK : (i + 1) * BLOCK] for i in range(3)] + [hid.at[2, pl.ds(0, LIVE)]]
+    csend = [xcb.at[:, 0:BLOCK], hid.at[2, pl.ds(0, LIVE)], wanted, hid.at[2, pl.ds(0, LIVE)]]
     ysend = [hid.at[i, pl.ds(0, LIVE)] for i in range(2)]
     yhalf = [hid.at[i, pl.ds(LIVE, HALF)] for i in range(2)]
 
@@ -193,6 +193,25 @@
         got(name, crecv.at[0, rows])
         yhalf[k][...] = (part[0, rows, :] + crecv[0, rows, :].astype(F32)).astype(BF16)
         send(there, yhalf[k], hrecv.at[k], device)
+
+    place = iota((BLOCK, BLOCK), 1)
+    source = ((place >> 5) & 3) * 128 + (place >> 7) * 32 + (place & 31)
+    perm[...] = (iota((BLOCK, BLOCK), 0) == source).astype(F32).astype(BF16)
+
+    settle("c0", "c0b")
+
+    @pl.loop(0, LIVE // 272)
+    def _(i):
+        rows = pl.ds(pl.multiple_of(i * 272, 16), 272)
+        for l in range(3):
+            whole_rows = jnp.concatenate(
+                [xc[rows, q * FEATS + l * 128 : q * FEATS + (l + 1) * 128] for q in range(4)], axis=1
+            )
+            swapped = jnp.dot(whole_rows, perm[...], preferred_element_type=F32).astype(BF16)
+            for q in range(4):
+                xcb[rows, q * FEATS + l * 128 : q * FEATS + (l + 1) * 128] = swapped[:, q * 128 : (q + 1) * 128]
+
+    exchange(1, xcb)
     to_sibling(1, 1)
     forward(y + 1, c, part.at[1])
     got("c1", crecv.at[1])
@@ -203,31 +222,13 @@
     got("c2", crecv.at[2])
     ysend[1][top, :] = (part[2, top, :] + crecv[2, top, :].astype(F32)).astype(BF16)
     send("f-a", ysend[1].at[top], frecv.at[1, top], down)
-
-    place = iota((BLOCK, BLOCK), 1)
-    source = ((place >> 5) & 3) * 128 + (place >> 7) * 32 + (place & 31)
-    perm[...] = (iota((BLOCK, BLOCK), 0) == source).astype(F32).astype(BF16)
-
-    settle("c0", "c0b", "c1", "c2")
-
-    @pl.loop(0, LIVE // 272)
-    def _(i):
-        rows = pl.ds(pl.multiple_of(i * 272, 16), 272)
-        for l in range(3):
-            whole_rows = jnp.concatenate(
-                [xc[rows, q * FEATS + l * 128 : q * FEATS + (l + 1) * 128] for q in range(4)], axis=1
-            )
-            swapped = jnp.dot(whole_rows, perm[...], preferred_element_type=F32).astype(BF16)
-            for q in range(4):
-                xcb[rows, q * FEATS + l * 128 : q * FEATS + (l + 1) * 128] = swapped[:, q * 128 : (q + 1) * 128]
-
-    exchange(1, xcb)
     got("h+", hrecv.at[0])
     ysend[0][top, :] = (part[1, top, :] + crecv[1, top, :].astype(F32) + hrecv[0].astype(F32)).astype(BF16)
     send("f+b", ysend[0].at[top], frecv.at[0, top], up)
     got("h-", hrecv.at[1])
     ysend[1][low, :] = (part[2, low, :] + crecv[2, low, :].astype(F32) + hrecv[1].astype(F32)).astype(BF16)
     send("f-b", ysend[1].at[low], frecv.at[1, low], down)
+    settle("c1", "c2")
     to_sibling(3, 0)
     forward(y, c, part.at[0])
     turned_expand = (iota((SLOTS, REQS), 0) >> 3 == iota((SLOTS, REQS), 1)).astype(F32).astype(BF16)
@@ -398,6 +399,8 @@
             rows = pl.ds(pl.multiple_of(((me[1 - h] + j) % 4) * ROWS_OUT, 32), ROWS_OUT)
             send(f"g{h}{b}{o}{j}", gs.at[h, rows, cols], gr.at[h, j - 1, :, cols], across(h, j))
 
+    turns = [(0, ALONG[h][1], 3, WHOLE[h]) for h in range(2)]
+
     def finish(h, b, o):
         column = block_of(b, o) * BLOCK + h * PART
         cols = pl.ds(pl.multiple_of(block_of(b, o) * PART, PART), PART)
@@ -416,7 +419,8 @@
             upd[l, :, wide] = new
             largest = jnp.maximum(largest, jnp.max(jnp.abs(new), axis=0, keepdims=True))
         for k in range(PART // 128):
-            mx[pl.ds(column // 128 + k, 1), :] = largest[:, k * 128 : (k + 1) * 128]
+            row = h * 4 + o * 2 + k
+            mxp[turns[h].index(b), row : row + 1, :] = largest[:, k * 128 : (k + 1) * 128]
 
     early = tuple(sent)
     for h in range(2):
@@ -431,7 +435,7 @@
     by_place = jnp.sum(jnp.where(hit, request_loss, 0.0), axis=1, keepdims=True)
     eye = iota((REQS, REQS), 0) == iota((REQS, REQS), 1)
     by_place = jnp.sum(jnp.where(eye, by_place, 0.0), axis=0, keepdims=True)
-    dpr[pl.ds(d, 1), 32:40, :] = jnp.broadcast_to(by_place[None], (1, 8, 128))
+    dpr[pl.ds(d, 1), 16:24, :] = jnp.broadcast_to(by_place[None], (1, 8, 128))
 
     settle(*early)
     for h in range(2):
@@ -492,6 +496,10 @@
     for h in range(2):
         for o in range(2):
             finish(h, ALONG[h][1], o)
+    dpr[pl.ds(d, 1), 0:8, :] = mxp[0:1]
+    dpr[pl.ds(d, 1), 8:16, :] = mxp[1:2]
+    for j in range(1, 16):
+        send(f"n{j}", dpr.at[d], dpr.at[d], {"tp": t, "dp": (d + j) % 16})
     for h in range(2):
         end_whole(h)
         grad(h, WHOLE[h], 0)
@@ -505,21 +513,37 @@
         for o in range(2):
             finish(h, WHOLE[h], o)
 
+    dpl[pl.ds(d, 1), 0:8, :] = mxp[2:3]
+    dpl[pl.ds(d, 1), 8:16, :] = mxp[3:4]
+    for j in range(1, 16):
+        send(f"o{j}", dpl.at[d], dpl.at[d], {"tp": t, "dp": (d + j) % 16})
+    for j in range(1, 16):
+        got(f"n{j}", dpr.at[(d + 16 - j) % 16])
+    over_dp = [dpr[0, 0:8, :], dpr[0, 8:16, :]]
+    for j in range(16):
+        for k in range(2):
+            over_dp[k] = jnp.maximum(over_dp[k], dpr[j, k * 8 : (k + 1) * 8, :])
+        sprd[j * 8 : (j + 1) * 8, :] = dpr[j, 16:24, :]
+    for j in range(1, 16):
+        got(f"o{j}", dpl.at[(d + 16 - j) % 16])
+    over_dp += [dpl[0, 0:8, :], dpl[0, 8:16, :]]
+    for j in range(1, 16):
+        for k in range(2):
+            over_dp[2 + k] = jnp.maximum(over_dp[2 + k], dpl[j, k * 8 : (k + 1) * 8, :])
+    for p in range(4):
+        for h in range(2):
+            for o in range(2):
+                first_row = block_of(turns[h][p], o) * 4 + h * 2
+                for k in range(2):
+                    row = h * 4 + o * 2 + k
+                    mx[pl.ds(first_row + k, 1), :] = over_dp[p][row : row + 1, :]
     for j in range(1, 8):
         send(f"m{j}", mx, mxr.at[j - 1], {"tp": (t + j) % 8, "dp": d})
-    settle(*(name for name in tuple(sent) if name[0] == "g"))
+    settle(*(name for name in tuple(sent) if name[0] != "m"))
     most = mx[...]
     for j in range(1, 8):
         got(f"m{j}", mxr.at[j - 1])
         most = jnp.maximum(most, mxr[j - 1])
-    dpr[pl.ds(d, 1), 0:32, :] = most[None]
-    for j in range(1, 16):
-        send(f"n{j}", dpr.at[d], dpr.at[d], {"tp": t, "dp": (d + j) % 16})
-    for j in range(1, 16):
-        got(f"n{j}", dpr.at[(d + 16 - j) % 16])
-    for j in range(16):
-        most = jnp.maximum(most, dpr[j, 0:32, :])
-        sprd[j * 8 : (j + 1) * 8, :] = dpr[j, 32:40, :]
     small_ref[0:32, :] = most + 1e-06
     lanes = iota((REQS, REQS), 1) == d * 8 + (iota((REQS, REQS), 0) & 7)
     mine = jnp.sum(jnp.where(lanes, sprd[...], 0.0), axis=1, keepdims=True)
@@ -570,9 +594,11 @@
             pltpu.VMEM((PAD, 128), F32),
             pltpu.VMEM((128, PAD), F32),
             pltpu.VMEM((8, 8, PAD), F32),
+            pltpu.VMEM((4, 8, 128), F32),
             pltpu.VMEM((32, 128), F32),
             pltpu.VMEM((7, 32, 128), F32),
-            pltpu.VMEM((16, 40, 128), F32),
+            pltpu.VMEM((16, 24, 128), F32),
+            pltpu.VMEM((16, 16, 128), F32),
             pltpu.VMEM((REQS, 128), F32),
             pltpu.SemaphoreType.DMA((18,)),
             pltpu.SemaphoreType.DMA((n,)),

time: 118 us -> 119 us (level)
    pallas_call x1, Pallas kernels: 115 us -> 116 us  [shards(): pl.pallas_call(kernel, out_shape=(jax.ShapeDtypeStruct((3, 32, OUT), F32)...]
where the time goes in v4:
time: 119 us
  Pallas kernels  118 us (99%)
    pallas_call x1, Pallas kernels, shards(): pl.pallas_call(kernel, out_shape=(jax.ShapeDtypeStruct((3, 32, OUT), F32)...  116 us
    pallas_call x1, Pallas kernels, shards(): pl.pallas_call(scaled, out_shape=(jax.ShapeDtypeStruct((1, REQS), F32), j...  2.47 us

profile of v4, /device:TPU:1, one launch (start us, length us, event | category | flops | bytes accessed | tf_op | source)
XLA Modules:
  0.0 119.1 jit_solution(8680401754918946525)
XLA Ops:
  0.6 116.0 %joining_step.1 = (f32[3,32,4096]{2,1,0:T(8,128)}, f32[40,128]{1,0:T(8,128)}) custom-call(bf16[3,1024,512]{2,1,0:T(8,128)(2,1)} %bitcast.6, bf16[1024,512]{1,0:T(8,128)(2,1)} %tgt_hbm.1, s32[1,128]{1,0:T(1,128)} %bitcast.8, s32[1,128]{1,0:T(1,128)} %bitcast.9, bf16[3,512,4096]{2,1,0:T(8,128)(2,1)} %w_hbm.1, f32[32,128]{1,0:T(8,128)} %bitcast.7), custom_call_target="tpu_custom_call" | custom-call | tf_op jit(solution)/shard_map/joining_step/pallas_call | solution.py:567
  116.7 2.5 %scaled.1 = (f32[1,128]{1,0:T(1,128)}, bf16[3,32,4096]{2,1,0:T(8,128)(2,1)}, f32[32,128]{1,0:T(8,128)}) custom-call(f32[3,32,4096]{2,1,0:T(8,128)} %get-tuple-element.8.upd, f32[40,128]{1,0:T(8,128)} %get-tuple-element.9.small), custom_call_target="tpu_custom_call" | custom-call | tf_op jit(solution)/shard_map/scaled/pallas_call | solution.py:619

commit v5 on v3

--- a/solution.py
+++ b/solution.py
@@ -82,16 +82,18 @@
 
     loads = [pltpu.make_async_copy(hid_hbm.at[l], hid.at[l], lsem.at[l]) for l in range(3)]
     loads.append(pltpu.make_async_copy(tgt_hbm, tgt, lsem.at[3]))
-    weights = []
-    for zz in range(4):
-        for l in range(3):
-            weights.append(
-                pltpu.make_async_copy(
-                    w_hbm.at[l, pl.ds(zz * 128, 128)],
-                    wv.at[pl.ds(zz * FEATS + l * 128, 128)],
-                    lsem.at[4 + zz * 3 + l],
+    weights = [[] for _ in range(4)]
+    for g, step in enumerate((2, 1, 3, 0)):
+        cols = pl.ds(pl.multiple_of(((y + step) % 4) * 2 * BLOCK, 2 * BLOCK), 2 * BLOCK)
+        for zz in range(4):
+            for l in range(3):
+                weights[g].append(
+                    pltpu.make_async_copy(
+                        w_hbm.at[l, pl.ds(zz * 128, 128), cols],
+                        wv.at[pl.ds(zz * FEATS + l * 128, 128), cols],
+                        lsem.at[4 + g * 12 + zz * 3 + l],
+                    )
                 )
-            )
     for load in loads[:3]:
         load.start()
     barrier = pltpu.get_barrier_semaphore()
@@ -125,7 +127,7 @@
     for load in loads[:3]:
         load.wait()
     loads[3].start()
-    for load in weights:
+    for load in weights[0]:
         load.start()
 
     @pl.loop(0, LIVE // 272)
@@ -138,6 +140,9 @@
                 cols = slice(q * FEATS + l * 128, q * FEATS + (l + 1) * 128)
                 xc[rows, cols] = got_rows[:, q * 128 : (q + 1) * 128]
 
+    for group in weights[1:]:
+        for load in group:
+            load.start()
     pl.semaphore_wait(barrier, 22)
 
     def feats(q):
@@ -157,12 +162,12 @@
         for j in (1, 2, 3):
             send(f"x{h}{j}", kept.at[:, feats(me[h] + j)], xg.at[h, rows_of(me[h]), :], axis(h, j))
         own_copies.append(
-            pltpu.make_async_copy(kept.at[:, feats(me[h])], xg.at[h, rows_of(me[h]), :], lsem.at[16 + h])
+            pltpu.make_async_copy(kept.at[:, feats(me[h])], xg.at[h, rows_of(me[h]), :], lsem.at[52 + h])
         )
         own_copies[h].start()
 
     exchange(0, xc)
-    for load in weights:
+    for load in weights[0]:
         load.wait()
 
     def forward(yy, core, dst, rows=slice(None)):
@@ -193,11 +198,15 @@
         got(name, crecv.at[0, rows])
         yhalf[k][...] = (part[0, rows, :] + crecv[0, rows, :].astype(F32)).astype(BF16)
         send(there, yhalf[k], hrecv.at[k], device)
+    for load in weights[1]:
+        load.wait()
     to_sibling(1, 1)
     forward(y + 1, c, part.at[1])
     got("c1", crecv.at[1])
     ysend[0][low, :] = (part[1, low, :] + crecv[1, low, :].astype(F32)).astype(BF16)
     send("f+a", ysend[0].at[low], frecv.at[0, low], up)
+    for load in weights[2]:
+        load.wait()
     to_sibling(2, 3)
     forward(y + 3, c, part.at[2])
     got("c2", crecv.at[2])
@@ -228,6 +237,8 @@
     got("h-", hrecv.at[1])
     ysend[1][low, :] = (part[2, low, :] + crecv[2, low, :].astype(F32) + hrecv[1].astype(F32)).astype(BF16)
     send("f-b", ysend[1].at[low], frecv.at[1, low], down)
+    for load in weights[3]:
+        load.wait()
     to_sibling(3, 0)
     forward(y, c, part.at[0])
     turned_expand = (iota((SLOTS, REQS), 0) >> 3 == iota((SLOTS, REQS), 1)).astype(F32).astype(BF16)
@@ -242,29 +253,37 @@
 
 
     got("c3", crecv.at[3])
+    stc[...] = jnp.zeros_like(stc)
+    lane = iota((CHUNK, 128), 1)
+
+    @pl.loop(0, LIVE // CHUNK)
+    def _(i):
+        rows = pl.ds(pl.multiple_of(i * CHUNK, CHUNK), CHUNK)
+        part[0, rows, :] = part[0, rows, :] + crecv[3, rows, :].astype(F32)
+        goal = wanted[rows, :].astype(F32)
+        row = jnp.where(lane == 3, jnp.sum(goal * goal, axis=1, keepdims=True), 0.0)
+        count = jnp.sum(owner[rows, :] * counts, axis=1, keepdims=True)
+        stc[rows, :] = jnp.where(lane == 4, count, row)
+
     got("f+a", frecv.at[0, low])
     got("f-a", frecv.at[1, top])
     got("f+b", frecv.at[0, top])
     got("f-b", frecv.at[1, low])
     gains = gain_ref[pl.ds(t * 4, 4), :]
     gain = jnp.concatenate([gains[k : k + 1, :] for k in range(4)], axis=1)
-    stc[...] = jnp.zeros_like(stc)
-    lane = iota((CHUNK, 128), 1)
 
     @pl.loop(0, LIVE // CHUNK)
     def _(i):
         rows = pl.ds(pl.multiple_of(i * CHUNK, CHUNK), CHUNK)
-        joined = part[0, rows, :] + crecv[3, rows, :].astype(F32)
-        joined = joined + (frecv[0, rows, :].astype(F32) + frecv[1, rows, :].astype(F32))
+        joined = part[0, rows, :] + (frecv[0, rows, :].astype(F32) + frecv[1, rows, :].astype(F32))
         part[0, rows, :] = joined
         goal = wanted[rows, :].astype(F32)
         scaled = joined * gain
-        sums = [joined * joined, scaled * scaled, scaled * goal, goal * goal]
-        row = jnp.zeros((CHUNK, 128), F32)
+        sums = [joined * joined, scaled * scaled, scaled * goal]
+        row = stc[rows, :]
         for k, term in enumerate(sums):
             row = jnp.where(lane == k, jnp.sum(term, axis=1, keepdims=True), row)
-        count = jnp.sum(owner[rows, :] * counts, axis=1, keepdims=True)
-        stc[rows, :] = jnp.where(lane == 4, count, row)
+        stc[rows, :] = row
 
     turned = stc[...].T
     count_row = jnp.maximum(turned[4:5, :], 1.0)
@@ -287,16 +306,18 @@
     str_[3:4, :] = row_loss
     stc[...] = str_[...].T
 
-    @pl.loop(0, LIVE // CHUNK)
-    def _(i):
-        rows = pl.ds(pl.multiple_of(i * CHUNK, CHUNK), CHUNK)
-        joined = part[0, rows, :]
-        stats = stc[rows, :]
-        err = joined * stats[:, 0:1] * gain - wanted[rows, :].astype(F32)
-        value = (stats[:, 1:2] * gain * err - joined * stats[:, 2:3]).astype(BF16)
-        for h in range(2):
+    def gradient(h):
+        cols = slice(h * PART, (h + 1) * PART)
+
+        @pl.loop(0, LIVE // CHUNK)
+        def _(i):
+            rows = pl.ds(pl.multiple_of(i * CHUNK, CHUNK), CHUNK)
             there = pl.ds(pl.multiple_of(me[h] * LIVE + i * CHUNK, CHUNK), CHUNK)
-            df[h, t, there, :] = value[:, h * PART : (h + 1) * PART]
+            joined = part[0, rows, cols]
+            stats = stc[rows, :]
+            err = joined * stats[:, 0:1] * gain[:, cols] - wanted[rows, cols].astype(F32)
+            value = stats[:, 1:2] * gain[:, cols] * err - joined * stats[:, 2:3]
+            df[h, t, there, :] = value.astype(BF16)
 
     def block(h, yy, place, half=None):
         start, size = (0, LIVE) if half is None else (half * HALF, HALF)
@@ -420,6 +441,7 @@
 
     early = tuple(sent)
     for h in range(2):
+        gradient(h)
         put_y(h, False)
         put_axis(h, 0)
 
@@ -574,7 +596,7 @@
             pltpu.VMEM((7, 32, 128), F32),
             pltpu.VMEM((16, 40, 128), F32),
             pltpu.VMEM((REQS, 128), F32),
-            pltpu.SemaphoreType.DMA((18,)),
+            pltpu.SemaphoreType.DMA((54,)),
             pltpu.SemaphoreType.DMA((n,)),
             pltpu.SemaphoreType.DMA((n,)),
         ],

time: 118 us -> 116 us (0.983)
  Pallas kernels: 117 us -> 115 us
    pallas_call x1, Pallas kernels: 115 us -> 113 us  [shards(): pl.pallas_call(kernel, out_shape=(jax.ShapeDtypeStruct((3, 32, OUT), F32)...]
where the time goes in v5:
time: 116 us
  Pallas kernels  115 us (99%)
    pallas_call x1, Pallas kernels, shards(): pl.pallas_call(kernel, out_shape=(jax.ShapeDtypeStruct((3, 32, OUT), F32)...  113 us
    pallas_call x1, Pallas kernels, shards(): pl.pallas_call(scaled, out_shape=(jax.ShapeDtypeStruct((1, REQS), F32), j...  2.47 us

profile of v5, /device:TPU:1, one launch (start us, length us, event | category | flops | bytes accessed | tf_op | source)
XLA Modules:
  0.0 115.9 jit_solution(15054320094299981078)
XLA Ops:
  0.6 112.8 %joining_step.1 = (f32[3,32,4096]{2,1,0:T(8,128)}, f32[40,128]{1,0:T(8,128)}) custom-call(bf16[3,1024,512]{2,1,0:T(8,128)(2,1)} %bitcast.6, bf16[1024,512]{1,0:T(8,128)(2,1)} %tgt_hbm.1, s32[1,128]{1,0:T(1,128)} %bitcast.8, s32[1,128]{1,0:T(1,128)} %bitcast.9, bf16[3,512,4096]{2,1,0:T(8,128)(2,1)} %w_hbm.1, f32[32,128]{1,0:T(8,128)} %bitcast.7), custom_call_target="tpu_custom_call" | custom-call | tf_op jit(solution)/shard_map/joining_step/pallas_call | solution.py:565
  113.4 2.5 %scaled.1 = (f32[1,128]{1,0:T(1,128)}, bf16[3,32,4096]{2,1,0:T(8,128)(2,1)}, f32[32,128]{1,0:T(8,128)}) custom-call(f32[3,32,4096]{2,1,0:T(8,128)} %get-tuple-element.8.upd, f32[40,128]{1,0:T(8,128)} %get-tuple-element.9.small), custom_call_target="tpu_custom_call" | custom-call | tf_op jit(solution)/shard_map/scaled/pallas_call | solution.py:615

commit v6 on v5

--- a/solution.py
+++ b/solution.py
@@ -86,14 +86,11 @@
     for g, step in enumerate((2, 1, 3, 0)):
         cols = pl.ds(pl.multiple_of(((y + step) % 4) * 2 * BLOCK, 2 * BLOCK), 2 * BLOCK)
         for zz in range(4):
-            for l in range(3):
-                weights[g].append(
-                    pltpu.make_async_copy(
-                        w_hbm.at[l, pl.ds(zz * 128, 128), cols],
-                        wv.at[pl.ds(zz * FEATS + l * 128, 128), cols],
-                        lsem.at[4 + g * 12 + zz * 3 + l],
-                    )
+            weights[g].append(
+                pltpu.make_async_copy(
+                    w_hbm.at[:, pl.ds(zz * 128, 128), cols], wv.at[zz, :, :, cols], lsem.at[4 + g * 4 + zz]
                 )
+            )
     for load in loads[:3]:
         load.start()
     barrier = pltpu.get_barrier_semaphore()
@@ -162,7 +159,7 @@
         for j in (1, 2, 3):
             send(f"x{h}{j}", kept.at[:, feats(me[h] + j)], xg.at[h, rows_of(me[h]), :], axis(h, j))
         own_copies.append(
-            pltpu.make_async_copy(kept.at[:, feats(me[h])], xg.at[h, rows_of(me[h]), :], lsem.at[52 + h])
+            pltpu.make_async_copy(kept.at[:, feats(me[h])], xg.at[h, rows_of(me[h]), :], lsem.at[20 + h])
         )
         own_copies[h].start()
 
@@ -177,7 +174,7 @@
         def _(i):
             cols = pl.ds(pl.multiple_of(column + i * PART, PART), PART)
             dst[rows, pl.ds(pl.multiple_of(i * PART, PART), PART)] = jnp.dot(
-                xc[rows, :], wv[:, cols], preferred_element_type=F32
+                xc[rows, :], wv[:, :, :, cols].reshape(4 * FEATS, PART), preferred_element_type=F32
             ).astype(dst.dtype)
 
     csend = [xcb.at[:, i * BLOCK : (i + 1) * BLOCK] for i in range(3)] + [hid.at[2, pl.ds(0, LIVE)]]
@@ -428,12 +425,12 @@
         largest = jnp.zeros((1, PART), F32)
         for l in range(3):
             mine = pl.ds(pl.multiple_of(me[1 - h] * ROWS_OUT + l * 32, 32), 32)
-            there = pl.ds(pl.multiple_of(z * FEATS + l * 128 + x * 32, 32), 32)
+            there = pl.ds(pl.multiple_of(x * 32, 32), 32)
             here = pl.ds(l * 32, 32)
             total = gs[h, mine, cols].astype(F32)
             for j in range(3):
                 total = total + gr[h, j, here, cols].astype(F32)
-            new = wv[there, wide].astype(F32) - learn_rate * total
+            new = wv[z, l, there, wide].astype(F32) - learn_rate * total
             upd[l, :, wide] = new
             largest = jnp.maximum(largest, jnp.max(jnp.abs(new), axis=0, keepdims=True))
         for k in range(PART // 128):
@@ -573,7 +570,7 @@
         scratch_shapes=[
             pltpu.VMEM((3, SLOTS, BLOCK), BF16),
             pltpu.VMEM((SLOTS, BLOCK), BF16),
-            pltpu.VMEM((4 * FEATS, OUT), BF16),
+            pltpu.VMEM((4, 3, 128, OUT), BF16),
             pltpu.VMEM((LIVE, SLOTS), BF16),
             pltpu.VMEM((BLOCK, BLOCK), BF16),
             pltpu.VMEM((LIVE, 4 * FEATS), BF16),
@@ -596,7 +593,7 @@
             pltpu.VMEM((7, 32, 128), F32),
             pltpu.VMEM((16, 40, 128), F32),
             pltpu.VMEM((REQS, 128), F32),
-            pltpu.SemaphoreType.DMA((54,)),
+            pltpu.SemaphoreType.DMA((22,)),
             pltpu.SemaphoreType.DMA((n,)),
             pltpu.SemaphoreType.DMA((n,)),
         ],

time: 116 us -> 116 us (level)
  no operation moved by 1% of the time
where the time goes in v6:
time: 116 us
  Pallas kernels  115 us (99%)
    pallas_call x1, Pallas kernels, shards(): pl.pallas_call(kernel, out_shape=(jax.ShapeDtypeStruct((3, 32, OUT), F32)...  112 us
    pallas_call x1, Pallas kernels, shards(): pl.pallas_call(scaled, out_shape=(jax.ShapeDtypeStruct((1, REQS), F32), j...  2.47 us

profile of v6, /device:TPU:1, one launch (start us, length us, event | category | flops | bytes accessed | tf_op | source)
XLA Modules:
  0.0 115.6 jit_solution(6927342545399588776)
XLA Ops:
  0.6 112.5 %joining_step.1 = (f32[3,32,4096]{2,1,0:T(8,128)}, f32[40,128]{1,0:T(8,128)}) custom-call(bf16[3,1024,512]{2,1,0:T(8,128)(2,1)} %bitcast.6, bf16[1024,512]{1,0:T(8,128)(2,1)} %tgt_hbm.1, s32[1,128]{1,0:T(1,128)} %bitcast.8, s32[1,128]{1,0:T(1,128)} %bitcast.9, bf16[3,512,4096]{2,1,0:T(8,128)(2,1)} %w_hbm.1, f32[32,128]{1,0:T(8,128)} %bitcast.7), custom_call_target="tpu_custom_call" | custom-call | tf_op jit(solution)/shard_map/joining_step/pallas_call | solution.py:562
  113.1 2.5 %scaled.1 = (f32[1,128]{1,0:T(1,128)}, bf16[3,32,4096]{2,1,0:T(8,128)(2,1)}, f32[32,128]{1,0:T(8,128)}) custom-call(f32[3,32,4096]{2,1,0:T(8,128)} %get-tuple-element.8.upd, f32[40,128]{1,0:T(8,128)} %get-tuple-element.9.small), custom_call_target="tpu_custom_call" | custom-call | tf_op jit(solution)/shard_map/scaled/pallas_call | solution.py:612

commit v7 on v5

--- a/solution.py
+++ b/solution.py
@@ -166,7 +166,6 @@
         )
         own_copies[h].start()
 
-    exchange(0, xc)
     for load in weights[0]:
         load.wait()
 
@@ -198,6 +197,7 @@
         got(name, crecv.at[0, rows])
         yhalf[k][...] = (part[0, rows, :] + crecv[0, rows, :].astype(F32)).astype(BF16)
         send(there, yhalf[k], hrecv.at[k], device)
+    exchange(0, xc)
     for load in weights[1]:
         load.wait()
     to_sibling(1, 1)

time: 116 us -> 116 us (level)
  no operation moved by 1% of the time
where the time goes in v7:
time: 116 us
  Pallas kernels  115 us (99%)
    pallas_call x1, Pallas kernels, shards(): pl.pallas_call(kernel, out_shape=(jax.ShapeDtypeStruct((3, 32, OUT), F32)...  113 us
    pallas_call x1, Pallas kernels, shards(): pl.pallas_call(scaled, out_shape=(jax.ShapeDtypeStruct((1, REQS), F32), j...  2.47 us

profile of v7, /device:TPU:1, one launch (start us, length us, event | category | flops | bytes accessed | tf_op | source)
XLA Modules:
  0.0 115.9 jit_solution(1649629452438269916)
XLA Ops:
  0.6 112.7 %joining_step.1 = (f32[3,32,4096]{2,1,0:T(8,128)}, f32[40,128]{1,0:T(8,128)}) custom-call(bf16[3,1024,512]{2,1,0:T(8,128)(2,1)} %bitcast.6, bf16[1024,512]{1,0:T(8,128)(2,1)} %tgt_hbm.1, s32[1,128]{1,0:T(1,128)} %bitcast.8, s32[1,128]{1,0:T(1,128)} %bitcast.9, bf16[3,512,4096]{2,1,0:T(8,128)(2,1)} %w_hbm.1, f32[32,128]{1,0:T(8,128)} %bitcast.7), custom_call_target="tpu_custom_call" | custom-call | tf_op jit(solution)/shard_map/joining_step/pallas_call | solution.py:565
  113.4 2.5 %scaled.1 = (f32[1,128]{1,0:T(1,128)}, bf16[3,32,4096]{2,1,0:T(8,128)(2,1)}, f32[32,128]{1,0:T(8,128)}) custom-call(f32[3,32,4096]{2,1,0:T(8,128)} %get-tuple-element.8.upd, f32[40,128]{1,0:T(8,128)} %get-tuple-element.9.small), custom_call_target="tpu_custom_call" | custom-call | tf_op jit(solution)/shard_map/scaled/pallas_call | solution.py:615
